TPU v7x, 512 devices: a whole 4x8x8 slice. The times are simulated.
512 devices in a mesh: img: 8 (over x, core), vol: 64 (over z, y).
Axes of the slice: x: 4, y: 8, z: 8, core: 2. Of those that a mesh axis runs over, the one named last changes fastest.
Arguments:
- density: float32 [256, 256, 256], P('vol', 'img'), may hold values from -6 to 6
- images: bfloat16 [4096, 2, 128, 256], P(('img', 'vol')), may hold values from -6 to 6
- block_tiles: int32 [2048, 128], P('img'), may hold values from 0 to 65535, as said below
- image_blocks: int32 [4096, 2], P(('img', 'vol')), may hold values from 0 to 3, all different within a row
- shifts: int32 [4096, 16], P(('img', 'vol')), may hold values from -8 to 8
- precision: float32 [4096], P(('img', 'vol')), may hold values from 0.002 to 0.02
Outputs:
- updated_map: float32 [256, 256, 2, 256], P('vol', 'img')
- posterior: float32 [4096, 2, 16], P(('img', 'vol'))
Inputs may be any that keep to these rules, and one draw needn't show every extreme that they name: `block_tiles`: entry q * 256 + p names the tile at (q, p). Row r of a block names p = 2 r or 2 r + 1, one of the two for the whole block. Among the entries of the 4 blocks of one device at most 16 have q in one slab of 4 values (q // 4 equal), and some device reaches 16 in every draw. `image_blocks`: each row names 2 different blocks.
All inputs are finite; a program needn't handle non-finite values.
Results may differ from a plain program's by a relative error of at most 0.005.
Values may be sent and summed in bfloat16 or wider, within the bound.
No kernel may reach another device: no remote copies, remote signals or barrier semaphores. Data moves between devices by JAX's collectives and lax.ppermute only.
A program may use at most 64 MiB of HBM per device.

v0:
```python
import functools
import math

import jax
import jax.numpy as jnp
import numpy as np
from jax import lax
from jax.experimental import pallas as pl
from jax.experimental.pallas import tpu as pltpu
from jax.sharding import PartitionSpec as P

N = 256
NG = 8
NV = 64
SLAB = 4
NB = 4
ROWS = 128
CAP = 16
FJ = N // NG
TR = 16
F32 = jnp.float32
BF = jnp.bfloat16
HI = lax.Precision.HIGHEST
VM = 100 * 1024 * 1024 // 2


def dot32(a, b):
    return jnp.dot(a, b, precision=HI, preferred_element_type=F32)


def dot16(a, b):
    return jnp.dot(a, b, preferred_element_type=F32)


def dot_nt(a, b, precision=None):
    return lax.dot_general(
        a, b, (((1,), (1,)), ((), ())), precision=precision, preferred_element_type=F32
    )


def lanes(shape):
    return lax.broadcasted_iota(jnp.int32, shape, len(shape) - 1)


def swap4(parts):
    group = lanes(parts[0].shape) // 32
    out = []
    for b in range(4):
        acc = None
        for a in range(4):
            shift = (32 * (a - b)) % 128
            moved = parts[a] if shift == 0 else pltpu.roll(parts[a], shift, 1)
            acc = moved if acc is None else jnp.where(group == a, moved, acc)
        out.append(acc)
    return out


def table_first():
    n = np.arange(N)
    ang = 2.0 * np.pi * ((n[:, None] * n[None, :]) % N) / N
    return np.concatenate([np.cos(ang), -np.sin(ang)], axis=1).astype(np.float32)


def table_second():
    k = np.arange(N).reshape(NV, SLAB)
    n = np.arange(N)
    ang = 2.0 * np.pi * ((k[:, :, None] * n[None, None, :]) % N) / N
    c, s = np.cos(ang), np.sin(ang)
    left = np.stack([c, -s], axis=1).reshape(2 * N, N)
    right = np.stack([s, c], axis=1).reshape(2 * N, N)
    return np.stack([left, right]).astype(np.float32)


def table_third():
    k = np.arange(N)
    n = (np.arange(NV)[None, :] * 4 + np.arange(4)[:, None]).reshape(-1)
    ang = 2.0 * np.pi * ((k[:, None] * n[None, :]) % N) / N
    scale = float(N) ** -1.5
    return np.stack([np.cos(ang) * scale, np.sin(ang) * scale]).astype(np.float32)


def table_fold():
    out = np.zeros((2, 4, 32, 2, 2, 32), np.float32)
    for c in range(2):
        for j in range(32):
            out[c, :, j, :, c, j] = 1.0
    return out.reshape(256, 128)


def table_spread():
    out = np.zeros((2, 2, 2, 32, 2, 4, 32), np.float32)
    for h in range(2):
        for c in range(2):
            for j in range(32):
                out[h, h, c, j, c, :, j] = 1.0
    return out.reshape(2, 128, 256)


def fill_lists(at_ref, tiles_ref, params_ref, o_ref):
    tiles = jnp.concatenate([tiles_ref[:, b, :] for b in range(NB)], axis=1)
    at = at_ref[0]
    width = NB * ROWS
    lane = lanes((NV, width))
    sub = lax.broadcasted_iota(jnp.int32, (NV, width), 0)
    earlier = jnp.where(
        lax.broadcasted_iota(jnp.int32, (width, width), 0) < lanes((width, width)), 1.0, 0.0
    ).astype(BF)

    owned = jnp.right_shift(tiles, 10) == at
    rank = dot16(jnp.where(owned, 1.0, 0.0).astype(BF), earlier).astype(jnp.int32)
    coded = jnp.bitwise_and(tiles, 1023) + jnp.right_shift(lane, 7) * 1024 + 1
    rank = jnp.where(owned, rank, -1)
    short = lanes((NV, 128))
    table = jnp.zeros((NV, 128), F32)
    for s in range(CAP):
        code = jnp.sum(jnp.where(rank == s, coded, 0).astype(F32), axis=1, keepdims=True)
        table = jnp.where(short == s, code, table)
    table = jnp.concatenate([table, table], axis=0) - 1.0
    codes = table.T[:CAP]

    mine = jnp.concatenate(
        [tiles_ref[pl.ds(at, 1), b, :] for b in range(NB)], axis=1
    )
    owner = jnp.right_shift(mine, 10)
    hot = sub == owner
    count = dot16(jnp.where(hot, 1.0, 0.0).astype(BF), earlier)
    place = jnp.sum(jnp.where(hot, count, 0.0), axis=0, keepdims=True).astype(jnp.int32)
    pos = owner * CAP + place
    row = lanes((8, width))
    kind = lax.broadcasted_iota(jnp.int32, (8, width), 0)
    digits = jnp.where(
        kind == 0, jnp.right_shift(row, 5), jnp.where(kind == 1, jnp.bitwise_and(row, 31), 1)
    ).astype(F32).astype(BF)
    found = jnp.where(
        lax.broadcasted_iota(jnp.int32, (NV * CAP, width), 0) == pos, 1.0, 0.0
    ).astype(BF)
    read = dot_nt(digits, found)
    inv = read[0:1] * 32.0 + read[1:2] + read[2:3] - 1.0
    pos = pos.astype(F32)
    params = params_ref[...]
    for k in range(NG):
        o_ref[k, 64:80] = codes
        for q in range(8):
            o_ref[k, 80 + q : 81 + q] = inv[:, q * 128 : q * 128 + 128]
        for q in range(4):
            o_ref[k, 88 + q : 89 + q] = pos[:, q * 128 : q * 128 + 128]
        o_ref[k, 92:96] = jnp.zeros((4, 128), F32)
        o_ref[k, 96:104] = params


def first_kernel(at_ref, d_ref, t_ref, tiles_ref, params_ref, o_ref):
    table = t_ref[...]
    rows = [dot32(d_ref[n0], table) for n0 in range(4)]
    for c in range(2):
        for hi in range(2):
            at = c * N + hi * 128
            moved = swap4([rows[n0][:, at : at + 128] for n0 in range(4)])
            for lo in range(4):
                o_ref[hi * 4 + lo, c * 32 : c * 32 + 32] = moved[lo]
    fill_lists(at_ref, tiles_ref, params_ref, o_ref)


def second_kernel(x_ref, w_ref, o_ref):
    re = x_ref[:, 0:32].reshape(N, 128)
    im = x_ref[:, 32:64].reshape(N, 128)
    o_ref[...] = (dot32(w_ref[0], re) + dot32(w_ref[1], im)).reshape(NV, 8, 128)


def slot_columns(lists_ref):
    low = lanes((CAP, 128)) < 64
    rows = [
        jnp.where(low, lists_ref[2 * gh, 64:80], lists_ref[2 * gh + 1, 64:80]) for gh in range(4)
    ]
    return jnp.concatenate(rows, axis=0).astype(jnp.int32)


def gather_kernel(x_ref, w_ref, fold_ref, lists_ref, f_ref, o_ref, half):
    parts = []
    for c in range(2):
        moved = swap4([x_ref[:, c * 4 + k, :] for k in range(4)])
        parts.append(jnp.concatenate(moved, axis=0))
    cos_t, sin_t = w_ref[0], w_ref[1]
    f_re = dot32(cos_t, parts[0]) + dot32(sin_t, parts[1])
    f_im = dot32(cos_t, parts[1]) - dot32(sin_t, parts[0])
    f_ref[0] = f_re
    f_ref[1] = f_im
    half[:, :128] = f_re.astype(BF)
    half[:, 128:] = f_im.astype(BF)

    columns = slot_columns(lists_ref)

    def step(nb, carry):
        cols = pltpu.roll(columns, 128 - 4 * nb, 1)
        tile = jnp.concatenate(
            [
                jnp.broadcast_to(cols[:, 64 * h + v : 64 * h + v + 1], (64, 128))
                for v in range(4)
                for h in range(2)
            ],
            axis=0,
        )
        lane = lanes(tile.shape)
        k0 = jnp.bitwise_and(tile, N - 1)
        k1 = jnp.where(tile < 0, -1, jnp.bitwise_and(jnp.right_shift(tile, 8), 3))
        hot = jnp.concatenate(
            [jnp.where(k0 == lane, 1.0, 0.0), jnp.where(k0 == lane + 128, 1.0, 0.0)], axis=1
        ).astype(BF)
        got = dot16(hot, half[...])
        keep = k1 == lane // 32
        kept = jnp.concatenate(
            [jnp.where(keep, got[:, :128], 0.0), jnp.where(keep, got[:, 128:], 0.0)], axis=1
        ).astype(BF)
        packed = dot16(kept, fold_ref[...]).reshape(4, 2, 64, 128)
        low = lanes((4, 64, 128)) < 64
        o_ref[pl.ds(nb * 4, 4)] = jnp.where(low, packed[:, 0], packed[:, 1]).astype(BF)
        return carry

    lax.fori_loop(0, 16, step, 0)


def image_kernel(x_ref, o_ref):
    for hi in range(2):
        parts = [
            x_ref[a // 2, a % 2, :, hi * 128 : hi * 128 + 128].astype(F32) for a in range(4)
        ]
        moved = swap4(parts)
        for lo in range(4):
            o_ref[hi * 4 + lo, 0] = moved[lo].astype(BF)


def score_kernel(x_ref, s_ref, lists_ref, t_ref, o_ref, cp1, cp2, ce):
    gh = pl.program_id(0)
    data = s_ref[...].reshape(NV * CAP, 128)
    half_of = lanes((512, 128)) // 64
    for h in range(2):
        g = gh * 2 + h
        inv = lists_ref[g, 80:88].astype(jnp.int32)
        sub = lax.broadcasted_iota(jnp.int32, (512, 128), 0)
        hot = jnp.concatenate(
            [jnp.where(sub == inv[q : q + 1], 1.0, 0.0).astype(BF) for q in range(8)], axis=1
        )
        got = dot16(hot, data)
        got = jnp.where(half_of == h, got, 0.0)
        rows = got + pltpu.roll(got, 64, 1)
        turned = pltpu.roll(rows, 32, 1)
        for b in range(NB):
            s_a = rows[b * ROWS : (b + 1) * ROWS]
            s_b = turned[b * ROWS : (b + 1) * ROWS]
            energy = jnp.sum(s_a * s_a, axis=0, keepdims=True)
            for ih in range(4):
                image = x_ref[h, ih].astype(F32)
                one = jnp.sum(s_a * image, axis=0, keepdims=True)
                two = jnp.sum(s_b * image, axis=0, keepdims=True)
                for lo in range(2):
                    at = pl.ds(g * 8 + lo * 4 + ih, 1)
                    cp1[b, at, :] = one
                    cp2[b, at, :] = two
                    ce[b, at, :] = energy

    @pl.when(gh == 3)
    def _():
        full = (
            dot32(cp1[...].reshape(256, 128), t_ref[0, 0])
            + dot32(cp2[...].reshape(256, 128), t_ref[0, 1])
            + dot32(ce[...].reshape(256, 128), jnp.full((128, 256), -0.25, F32))
        ).reshape(NB, 64, 256)
        group = lanes((64, 128)) // 32
        first = lax.broadcasted_iota(jnp.int32, (64, 128), 0) % 8 < 4
        table = jnp.zeros((64, 128), F32)
        for b in range(NB):
            own = jnp.where(first, full[b, :, :128], full[b, :, 128:])
            table = jnp.where(group == b, own, table)
        idx = lists_ref[:, 96:104].reshape(64, 128).astype(jnp.int32)
        score = jnp.take_along_axis(table, jnp.bitwise_and(idx, 127), axis=1)
        group = lanes((16, 128)) // 32
        packed = score[:16]
        for q in range(1, 4):
            packed = jnp.where(group == q, pltpu.roll(score[q * 16 : q * 16 + 16], 32 * q, 1), packed)
        for k in range(NG):
            o_ref[k] = packed


def back_kernel(x_ref, p_ref, lists_ref, u_ref, w_ref, o_ref, fr, fi, rows):
    gh = pl.program_id(0)

    @pl.when(gh == 0)
    def _():
        packed = p_ref[0]
        for k in range(1, NG):
            packed = packed + p_ref[k]
        score = jnp.concatenate(
            [packed if q == 0 else pltpu.roll(packed, 128 - 32 * q, 1) for q in range(4)], axis=0
        )
        lane = lanes((64, 128))
        valid = lane < 2 * TR
        params = lists_ref[:, 96:104].reshape(64, 128)
        logits = score * params[:, 32:33]
        top = jnp.max(jnp.where(valid, logits, -jnp.inf), axis=1, keepdims=True)
        expo = jnp.where(valid, jnp.exp(jnp.where(valid, logits - top, 0.0)), 0.0)
        post = expo / jnp.sum(expo, axis=1, keepdims=True)
        w_ref[...] = post
        idx = params.astype(jnp.int32)
        weight = jnp.zeros((64, 128), F32)
        for k in range(2 * TR):
            weight = weight + jnp.where(lane == idx[:, k : k + 1], post[:, k : k + 1], 0.0)
        group = lane // 32
        stacked = jnp.concatenate(
            [jnp.where(group == b, weight, 0.0) for b in range(NB)], axis=0
        )
        fac = dot32(stacked, u_ref[0]).reshape(NB, 64, 256)
        low = lane < 64
        for b in range(NB):
            for part, ref in ((0, fr), (1, fi)):
                val = fac[b, :, part * 128 : part * 128 + 128]
                val = jnp.where(low, val, pltpu.roll(val, 60, 0))
                ref[b] = val.astype(BF).astype(F32)
        block_of = (
            lanes((8, 128)) // 32 == lax.broadcasted_iota(jnp.int32, (8, 128), 0)
        ).astype(F32)
        per_image = dot_nt(block_of, weight, HI)
        sub = lax.broadcasted_iota(jnp.int32, (64, 128), 0)
        per_group = dot32(per_image, (sub // 8 == lane % 32 // 4).astype(F32))
        sub = lax.broadcasted_iota(jnp.int32, (8, 128), 0)
        lane = lanes((8, 128))
        mass = jnp.sum(jnp.where(sub == lane % 4, per_group, 0.0), axis=0, keepdims=True)
        upper = mass.astype(BF).astype(F32)
        middle = (mass - upper).astype(BF).astype(F32)
        piece = lanes((1, 128)) // 32
        mass = jnp.where(
            piece == 0,
            upper,
            jnp.where(piece == 1, middle, jnp.where(piece == 2, mass - upper - middle, 0.0)),
        )
        o_ref[:, 64:72] = jnp.broadcast_to(mass.reshape(1, 1, 128), (NV, 8, 128)).astype(BF)

    low = lanes((NV * CAP, 128)) < 64
    outs = []
    for h in range(2):
        g = gh * 2 + h
        for b in range(NB):
            acc_a = jnp.zeros((ROWS, 128), F32)
            acc_b = jnp.zeros((ROWS, 128), F32)
            for ih in range(4):
                image = x_ref[h, ih].astype(F32)
                at = pl.ds(g * 8 + ih, 1)
                acc_a = acc_a + image * fr[b, at, :]
                acc_b = acc_b + image * fi[b, at, :]
            acc = acc_a + pltpu.roll(acc_a, 64, 1)
            acc_b = acc_b + pltpu.roll(acc_b, 64, 1)
            rows[b * ROWS : (b + 1) * ROWS] = (acc + pltpu.roll(acc_b, 32, 1)).astype(BF)
        pos = lists_ref[g, 88:92].astype(jnp.int32)
        sub = lax.broadcasted_iota(jnp.int32, (NV * CAP, 128), 0)
        hot = jnp.concatenate(
            [jnp.where(sub == pos[q : q + 1], 1.0, 0.0).astype(BF) for q in range(4)], axis=1
        )
        outs.append(dot16(hot, rows[...]))
    at = pl.ds(pl.multiple_of(gh * CAP, CAP), CAP)
    o_ref[:, at, :] = jnp.where(low, outs[0], outs[1]).astype(BF).reshape(NV, CAP, 128)


def total_kernel(x_ref, f_ref, spread_ref, lists_ref, o_ref, tot, msum, codes, slot_mass):
    tot[...] = jnp.zeros_like(tot)
    msum[...] = jnp.zeros_like(msum)
    columns = slot_columns(lists_ref)
    by_slot = jnp.concatenate(
        [lists_ref[2 * gh + h, 64:80] for h in range(2) for gh in range(4)], axis=0
    )
    code = by_slot.T[:NV].astype(jnp.int32)
    codes[...] = code
    sent = x_ref[:, 64:72, :].astype(F32)[:, 0, :]
    source = lax.broadcasted_iota(jnp.int32, (128, 128), 0)
    target = lanes((128, 128))
    group = target % 64 // 16 * 2 + target // 64
    mass = jnp.zeros((NV, 128), F32)
    for b in range(NB):
        pick = (source % 32 == group * 4 + b).astype(F32)
        mass = jnp.where(jnp.right_shift(code, 10) == b, dot32(sent, pick), mass)
    slot_mass[...] = mass

    def step(nb, carry):
        cols = pltpu.roll(columns, 128 - 4 * nb, 1)
        data = x_ref[pl.ds(nb * 4, 4), 0:64, :].reshape(256, 128)
        kept = []
        for h in range(2):
            col = jnp.concatenate(
                [
                    jnp.broadcast_to(cols[:, 64 * h + v : 64 * h + v + 1], (64, 128))
                    for v in range(4)
                ],
                axis=0,
            )
            k1 = jnp.where(col < 0, -1, jnp.bitwise_and(jnp.right_shift(col, 8), 3))
            keep = k1 == lanes((256, 128)) // 32
            wide = dot16(data, spread_ref[h])
            kept.append(
                jnp.concatenate(
                    [jnp.where(keep, wide[:, :128], 0.0), jnp.where(keep, wide[:, 128:], 0.0)],
                    axis=1,
                ).astype(BF)
            )
        kept = jnp.concatenate(
            [kept[h][v * 64 : v * 64 + 64] for v in range(4) for h in range(2)], axis=0
        )
        hots, weights = [], []
        for v in range(4):
            at = pl.ds(nb * 4 + v, 1)
            row = codes[at, :]
            mass = slot_mass[at, :]
            hots.append(
                jnp.where(
                    lax.broadcasted_iota(jnp.int32, (N, 128), 0) == jnp.bitwise_and(row, N - 1),
                    1.0,
                    0.0,
                ).astype(BF)
            )
            sub = lax.broadcasted_iota(jnp.int32, (8, 128), 0)
            hit = (sub % 4 == jnp.bitwise_and(jnp.right_shift(row, 8), 3)) & (row >= 0)
            upper = mass.astype(BF).astype(F32)
            weights.append(
                jnp.where(hit, jnp.where(sub < 4, upper, mass - upper), 0.0).astype(BF)
            )
        hot = jnp.concatenate(hots, axis=1)
        tot[...] += dot16(hot, kept)
        msum[...] += dot_nt(hot, jnp.concatenate(weights, axis=1))
        return carry

    lax.fori_loop(0, 16, step, 0)
    expand = (
        lanes((8, 128)) // 32 == lax.broadcasted_iota(jnp.int32, (8, 128), 0) % 4
    ).astype(F32)
    scale = 1.0 / (1.0 + dot32(msum[...], expand))
    for c in range(2):
        new = (tot[:, c * 128 : c * 128 + 128] + f_ref[c]) * scale
        o_ref[:, c] = new.reshape(NG, FJ, 128)


def last_kernel(x_ref, o_ref):
    for c in range(2):
        for hi in range(2):
            moved = swap4([x_ref[hi * 4 + lo, c] for lo in range(4)])
            for k in range(4):
                o_ref[k, :, c, hi * 128 : hi * 128 + 128] = moved[k]


def call(kernel, out, name, **extra):
    return pl.pallas_call(
        kernel,
        out_shape=out,
        name=name,
        compiler_params=pltpu.CompilerParams(vmem_limit_bytes=VM),
        **extra,
    )


def struct(shape, dtype=F32):
    return jax.ShapeDtypeStruct(shape, dtype)


def over_img(x):
    return lax.all_to_all(x, "img", split_axis=0, concat_axis=0, tiled=True)


def over_vol(x):
    return lax.all_to_all(x, "vol", split_axis=0, concat_axis=0, tiled=True)


def phase_tables():
    freq = np.arange(N).reshape(NG, FJ)
    shift = np.arange(32) - 8
    ang = 2.0 * np.pi * ((freq[:, :, None] * shift[None, None, :]) % N) / N
    cos_t, sin_t = np.cos(ang), np.sin(ang)
    score = np.zeros((NG, 2, 2, 2, FJ, 2, NB, 32), np.float32)
    back = np.zeros((NG, NB, 32, 2, 2, 2, FJ), np.float32)
    for c in range(2):
        sign = 1.0 if c else -1.0
        for lo in range(2):
            score[:, 0, lo, c, :, lo] = cos_t[:, :, None, :]
            score[:, 1, lo, c, :, lo] = sign * sin_t[:, :, None, :]
            back[:, :, :, 0, lo, c, :] = cos_t.transpose(0, 2, 1)[:, None]
            back[:, :, :, 1, lo, c, :] = sign * sin_t.transpose(0, 2, 1)[:, None]
    return score.reshape(NG, 2, 128, 256), back.reshape(NG, 128, 256)


def per_device(density, images, block_tiles, image_blocks, shifts, precision):
    vol_at = lax.axis_index("vol")
    img_at = lax.axis_index("img")
    score_t, back_t = phase_tables()
    score_t = lax.dynamic_slice_in_dim(jnp.asarray(score_t), img_at, 1, 0)
    back_t = lax.dynamic_slice_in_dim(jnp.asarray(back_t), img_at, 1, 0)
    smem = pl.BlockSpec(memory_space=pltpu.SMEM)
    vmem = pl.BlockSpec(memory_space=pltpu.VMEM)

    idx = (image_blocks[:, :, None] * 32 + shifts[:, None, :] + 8).reshape(NG, 2 * TR)
    params = jnp.concatenate(
        [idx.astype(F32), precision[:, None], jnp.zeros((NG, 127 - 2 * TR), F32)], axis=1
    )
    params = params.reshape(4, 2, 128).transpose(1, 0, 2).reshape(8, 128)

    one = call(
        first_kernel,
        struct((NG, 104, 128)),
        "third_index",
        in_specs=[smem, vmem, vmem, vmem, vmem],
    )(
        vol_at.reshape(1).astype(jnp.int32),
        density,
        table_first(),
        block_tiles.reshape(NV, NB, ROWS),
        params,
    )
    images, one = lax.optimization_barrier((images, one))
    lists = over_img(one)

    shared = call(
        image_kernel,
        struct((NG, 4, ROWS, 128), BF),
        "image_split",
        grid=(4,),
        in_specs=[pl.BlockSpec((2, 2, ROWS, N), lambda i: (i, 0, 0, 0))],
        out_specs=pl.BlockSpec((NG, 1, ROWS, 128), lambda i: (0, i, 0, 0)),
    )(images)
    lists, shared = lax.optimization_barrier((lists, shared))
    two = call(second_kernel, struct((NV, 8, 128)), "second_index")(lists, table_second())
    two = over_vol(two)
    two, shared = lax.optimization_barrier((two, shared))
    shared = over_img(shared)

    fourier, outgoing = call(
        gather_kernel,
        (struct((2, N, 128)), struct((NV, 64, 128), BF)),
        "slice_tiles",
        scratch_shapes=[pltpu.VMEM((N, N), BF)],
    )(two, table_third(), jnp.asarray(table_fold(), BF), lists)
    incoming = over_vol(outgoing).reshape(NV, 4, CAP, 128)

    def whole_spec(shape):
        return pl.BlockSpec(shape, lambda i: (0,) * len(shape))

    image_spec = pl.BlockSpec((2, 4, ROWS, 128), lambda i: (i, 0, 0, 0))
    slot_spec = pl.BlockSpec((NV, 1, CAP, 128), lambda i: (0, i, 0, 0))
    partial = call(
        score_kernel,
        struct((NG, 16, 128)),
        "score",
        grid=(4,),
        in_specs=[
            image_spec,
            slot_spec,
            whole_spec((NG, 104, 128)),
            whole_spec((1, 2, 128, 256)),
        ],
        out_specs=whole_spec((NG, 16, 128)),
        scratch_shapes=[pltpu.VMEM((NB, 64, 128), F32)] * 3,
    )(shared, incoming, lists, score_t)
    partial = over_img(partial)

    weights, back = call(
        back_kernel,
        (struct((64, 128)), struct((NV, 72, 128), BF)),
        "backproject",
        grid=(4,),
        in_specs=[
            image_spec,
            whole_spec((NG, 16, 128)),
            whole_spec((NG, 104, 128)),
            whole_spec((1, 128, 256)),
        ],
        out_specs=(whole_spec((64, 128)), whole_spec((NV, 72, 128))),
        scratch_shapes=[
            pltpu.VMEM((NB, 64, 128), F32),
            pltpu.VMEM((NB, 64, 128), F32),
            pltpu.VMEM((512, 128), BF),
        ],
    )(shared, partial, lists, back_t)
    returned = over_vol(back)

    updated = call(
        total_kernel,
        struct((NG, 2, FJ, 128)),
        "totals",
        scratch_shapes=[
            pltpu.VMEM((N, N), F32),
            pltpu.VMEM((N, 8), F32),
            pltpu.VMEM((NV, 128), jnp.int32),
            pltpu.VMEM((NV, 128), F32),
        ],
    )(returned, fourier, jnp.asarray(table_spread(), BF), lists)
    updated = over_img(updated)
    updated = call(last_kernel, struct((SLAB, FJ, 2, N)), "frequency_join")(updated)

    own = lax.dynamic_slice_in_dim(weights, img_at * 8, 8, 0)[:, : 2 * TR]
    posterior = own.reshape(2, 4, 2, TR).transpose(1, 0, 2, 3).reshape(NG, 2, TR)
    return (updated, posterior)


def solution(mesh):
    in_specs = (
        P("vol", "img", None),
        P(("img", "vol"), None, None, None),
        P("img", None),
        P(("img", "vol"), None),
        P(("img", "vol"), None),
        P(("img", "vol")),
    )
    out_specs = (P("vol", "img", None, None), P(("img", "vol"), None, None))
    return jax.shard_map(
        per_device, mesh=mesh, in_specs=in_specs, out_specs=out_specs, check_vma=False
    )
```

profile of v0, /device:TPU:1, one launch (start us, length us, event | category | flops | bytes accessed | tf_op | source)
XLA Modules:
  0.0 189.6 jit_solution(5518359364371822610)
XLA Ops:
  0.6 0.8 concatenate.6
  1.5 0.1 copy.20
  1.6 0.7 broadcast_multiply_fusion
  2.3 0.8 add_convert_fusion
  3.1 0.1 convert_element_type.8
  3.4 1.1 copy-done.4
  4.5 0.9 copy-done.5
  5.4 0.9 copy-done.6
  6.3 2.8 %third_index.1 = f32[8,104,128]{2,1,0:T(8,128)} custom-call(s32[1]{0:T(128)} %bitcast.at_ref, f32[4,32,256]{2,1,0:T(8,128)S(1)} %copy-done.5, f32[256,512]{1,0:T(8,128)S(1)} %copy-done.4, s32[64,4,128]{2,1,0:T(4,128)S(1)} %bitcast.10, f32[8,128]{1,0:T(8,128)S(1)} %bitcast.11), custom_call_target="tpu_custom_call" | custom-call | tf_op jit(solution)/shard_map/third_index/pallas_call | solution.py:499
  9.1 10.2 %all-to-all-start = ((f32[8,104,128]{2,1,0:T(8,128)}), f32[8,104,128]{2,1,0:T(8,128)S(1)}, u32[]{:S(2)}, u32[]{:S(2)}) async-start(f32[8,104,128]{2,1,0:T(8,128)} %third_index.1), calls=%async_computation | async-start | bytes 851968 | tf_op jit(solution)/shard_map/all_to_all | solution.py:460
  19.3 2.3 %image_split.1 = bf16[8,4,128,128]{3,2,1,0:T(8,128)(2,1)} custom-call(bf16[8,2,128,256]{3,2,1,0:T(8,128)(2,1)S(1)} %copy-done), custom_call_target="tpu_custom_call" | custom-call | tf_op jit(solution)/shard_map/image_split/pallas_call | solution.py:514
  21.6 6.1 %all-to-all-done.x_ref.lists_ref = f32[8,104,128]{2,1,0:T(8,128)S(1)} async-done(((f32[8,104,128]{2,1,0:T(8,128)}), f32[8,104,128]{2,1,0:T(8,128)S(1)}, u32[]{:S(2)}, u32[]{:S(2)}) %all-to-all-start) | async-done | bytes 426016 | tf_op jit(solution)/shard_map/all_to_all | solution.py:460
  27.8 1.0 second_index.1
  28.8 24.2 %all_to_all.35.x_ref = f32[64,8,128]{2,1,0:T(8,128)S(1)} all-to-all(f32[64,8,128]{2,1,0:T(8,128)S(1)} %second_index.1), channel_id=1, replica_groups=mesh['img'=8,'vol'=64] {'vol'}, dimensions={0} | all-to-all | bytes 524288 | tf_op jit(solution)/shard_map/all_to_all | solution.py:464
  53.0 6.8 %all-to-all-start.2 = ((bf16[8,4,128,128]{3,2,1,0:T(8,128)(2,1)}), bf16[8,4,128,128]{3,2,1,0:T(8,128)(2,1)S(1)}, u32[]{:S(2)}, u32[]{:S(2)}) async-start(bf16[8,4,128,128]{3,2,1,0:T(8,128)(2,1)} %image_split.1), calls=%async_computation.2 | async-start | bytes 2097152 | tf_op jit(solution)/shard_map/all_to_all | solution.py:460
  59.9 9.4 %slice_tiles.1 = (f32[2,256,128]{2,1,0:T(8,128)S(1)}, bf16[64,64,128]{2,1,0:T(8,128)(2,1)S(1)}) custom-call(f32[64,8,128]{2,1,0:T(8,128)S(1)} %all_to_all.35.x_ref, f32[2,256,256]{2,1,0:T(8,128)S(1)} %copy-done.3, bf16[256,128]{1,0:T(8,128)(2,1)S(1)} %copy-done.8, f32[8,104,128]{2,1,0:T(8,128)S(1)} %all-to-all-done.x_ref.lists_ref), custom_call_target="tpu_custom_call" | custom-call | tf_op jit(solution)/shard_map/slice_tiles/pallas_call | solution.py:528
  69.2 1.0 copy-done.2
  70.2 4.7 %all-to-all-done.2.x_ref = bf16[8,4,128,128]{3,2,1,0:T(8,128)(2,1)S(1)} async-done(((bf16[8,4,128,128]{3,2,1,0:T(8,128)(2,1)}), bf16[8,4,128,128]{3,2,1,0:T(8,128)(2,1)S(1)}, u32[]{:S(2)}, u32[]{:S(2)}) %all-to-all-start.2) | async-done | bytes 1048608 | tf_op jit(solution)/shard_map/all_to_all | solution.py:460
  75.0 4.7 %all-to-all-start.3 = ((bf16[64,64,128]{2,1,0:T(8,128)(2,1)}), bf16[64,64,128]{2,1,0:T(8,128)(2,1)S(1)}, u32[]{:S(2)}, u32[]{:S(2)}) async-start(bf16[64,64,128]{2,1,0:T(8,128)(2,1)} %copy-done.2), calls=%async_computation.3 | async-start | bytes 2097152 | tf_op jit(solution)/shard_map/all_to_all | solution.py:464
  79.6 1.0 constant_dynamic-slice_fusion.2.t_ref
  80.6 26.5 %all-to-all-done.3 = bf16[64,64,128]{2,1,0:T(8,128)(2,1)S(1)} async-done(((bf16[64,64,128]{2,1,0:T(8,128)(2,1)}), bf16[64,64,128]{2,1,0:T(8,128)(2,1)S(1)}, u32[]{:S(2)}, u32[]{:S(2)}) %all-to-all-start.3) | async-done | bytes 1048608 | tf_op jit(solution)/shard_map/all_to_all | solution.py:464
  107.1 6.2 %score.1 = f32[8,16,128]{2,1,0:T(8,128)} custom-call(bf16[8,4,128,128]{3,2,1,0:T(8,128)(2,1)S(1)} %all-to-all-done.2.x_ref, bf16[64,4,16,128]{3,2,1,0:T(8,128)(2,1)S(1)} %bitcast.9, f32[8,104,128]{2,1,0:T(8,128)S(1)} %all-to-all-done.x_ref.lists_ref, f32[1,2,128,256]{3,2,1,0:T(8,128)S(1)} %constant_dynamic-slice_fusion.2.t_ref), custom_call_target="tpu_custom_call" | custom-call | tf_op jit(solution)/shard_map/score/pallas_call | solution.py:541
  113.3 6.6 %all-to-all-start.4 = ((f32[8,16,128]{2,1,0:T(8,128)}), f32[8,16,128]{2,1,0:T(8,128)S(1)}, u32[]{:S(2)}, u32[]{:S(2)}) async-start(f32[8,16,128]{2,1,0:T(8,128)} %score.1), calls=%async_computation.4 | async-start | bytes 131072 | tf_op jit(solution)/shard_map/all_to_all | solution.py:460
  119.9 0.9 constant_dynamic-slice_fusion.1.u_ref
  120.8 3.9 %all-to-all-done.4.p_ref = f32[8,16,128]{2,1,0:T(8,128)S(1)} async-done(((f32[8,16,128]{2,1,0:T(8,128)}), f32[8,16,128]{2,1,0:T(8,128)S(1)}, u32[]{:S(2)}, u32[]{:S(2)}) %all-to-all-start.4) | async-done | bytes 65568 | tf_op jit(solution)/shard_map/all_to_all | solution.py:460
  124.7 5.8 %backproject.1 = (f32[64,128]{1,0:T(8,128)S(1)}, bf16[64,72,128]{2,1,0:T(8,128)(2,1)S(1)}) custom-call(bf16[8,4,128,128]{3,2,1,0:T(8,128)(2,1)S(1)} %all-to-all-done.2.x_ref, f32[8,16,128]{2,1,0:T(8,128)S(1)} %all-to-all-done.4.p_ref, f32[8,104,128]{2,1,0:T(8,128)S(1)} %all-to-all-done.x_ref.lists_ref, f32[1,128,256]{2,1,0:T(8,128)S(1)} %constant_dynamic-slice_fusion.1.u_ref), custom_call_target="tpu_custom_call" | custom-call | tf_op jit(solution)/shard_map/backproject/pallas_call | solution.py:557
  130.5 35.8 %all_to_all.36.x_ref = bf16[64,72,128]{2,1,0:T(8,128)(2,1)S(1)} all-to-all(bf16[64,72,128]{2,1,0:T(8,128)(2,1)S(1)} %get-tuple-element.19), channel_id=1, replica_groups=mesh['img'=8,'vol'=64] {'vol'}, dimensions={0} | all-to-all | bytes 2359296 | tf_op jit(solution)/shard_map/all_to_all | solution.py:464
  166.3 8.7 %totals.1 = f32[8,2,32,128]{3,2,1,0:T(8,128)} custom-call(bf16[64,72,128]{2,1,0:T(8,128)(2,1)S(1)} %all_to_all.36.x_ref, f32[2,256,128]{2,1,0:T(8,128)S(1)} %get-tuple-element.20.f_ref, bf16[2,128,256]{2,1,0:T(8,128)(2,1)S(1)} %copy-done.7, f32[8,104,128]{2,1,0:T(8,128)S(1)} %all-to-all-done.x_ref.lists_ref), custom_call_target="tpu_custom_call" | custom-call | tf_op jit(solution)/shard_map/totals/pallas_call | solution.py:577
  175.1 7.0 %all-to-all-start.6 = ((f32[8,2,32,128]{3,2,1,0:T(8,128)}), f32[8,2,32,128]{3,2,1,0:T(8,128)S(1)}, u32[]{:S(2)}, u32[]{:S(2)}) async-start(f32[8,2,32,128]{3,2,1,0:T(8,128)} %totals.1), calls=%async_computation.6 | async-start | bytes 524288 | tf_op jit(solution)/shard_map/all_to_all | solution.py:460
  182.1 0.6 copy.21
  182.7 5.8 %all-to-all-done.6.x_ref = f32[8,2,32,128]{3,2,1,0:T(8,128)S(1)} async-done(((f32[8,2,32,128]{3,2,1,0:T(8,128)}), f32[8,2,32,128]{3,2,1,0:T(8,128)S(1)}, u32[]{:S(2)}, u32[]{:S(2)}) %all-to-all-start.6) | async-done | bytes 262176 | tf_op jit(solution)/shard_map/all_to_all | solution.py:460
  188.6 1.0 frequency_join.1
  (21 shorter events, 0.4 us)
Async XLA Ops:
  0.6 18.7 %copy-start = (bf16[8,2,128,256]{3,2,1,0:T(8,128)(2,1)S(1)}, bf16[8,2,128,256]{3,2,1,0:T(8,128)(2,1)}, u32[]{:S(2)}) copy-start(bf16[8,2,128,256]{3,2,1,0:T(8,128)(2,1)} %x_ref) | copy-start | bytes 3145732
  3.2 24.6 %copy-start.1 = (f32[2,512,256]{2,1,0:T(8,128)S(1)}, f32[2,512,256]{2,1,0:T(8,128)}, u32[]{:S(2)}) copy-start(f32[2,512,256]{2,1,0:T(8,128)} %constant.37.clone.w_ref) | copy-start | bytes 3145732
  3.4 1.1 copy-start.4
  4.5 0.9 copy-start.5
  5.4 0.9 copy-start.6
  9.1 18.7 %all-to-all-start = ((f32[8,104,128]{2,1,0:T(8,128)}), f32[8,104,128]{2,1,0:T(8,128)S(1)}, u32[]{:S(2)}, u32[]{:S(2)}) async-start(f32[8,104,128]{2,1,0:T(8,128)} %third_index.1), calls=%async_computation | async-start | bytes 851968 | tf_op jit(solution)/shard_map/all_to_all | solution.py:460
  21.6 38.2 %copy-start.3 = (f32[2,256,256]{2,1,0:T(8,128)S(1)}, f32[2,256,256]{2,1,0:T(8,128)}, u32[]{:S(2)}) copy-start(f32[2,256,256]{2,1,0:T(8,128)} %constant.39.clone.w_ref) | copy-start | bytes 1572868
  21.6 38.2 %copy-start.8 = (bf16[256,128]{1,0:T(8,128)(2,1)S(1)}, bf16[256,128]{1,0:T(8,128)(2,1)}, u32[]{:S(2)}) copy-start(bf16[256,128]{1,0:T(8,128)(2,1)} %constant.38.clone.fold_ref) | copy-start | bytes 196612
  53.0 21.9 %all-to-all-start.2 = ((bf16[8,4,128,128]{3,2,1,0:T(8,128)(2,1)}), bf16[8,4,128,128]{3,2,1,0:T(8,128)(2,1)S(1)}, u32[]{:S(2)}, u32[]{:S(2)}) async-start(bf16[8,4,128,128]{3,2,1,0:T(8,128)(2,1)} %image_split.1), calls=%async_computation.2 | async-start | bytes 2097152 | tf_op jit(solution)/shard_map/all_to_all | solution.py:460
  69.2 1.0 copy-start.2
  75.0 32.1 %all-to-all-start.3 = ((bf16[64,64,128]{2,1,0:T(8,128)(2,1)}), bf16[64,64,128]{2,1,0:T(8,128)(2,1)S(1)}, u32[]{:S(2)}, u32[]{:S(2)}) async-start(bf16[64,64,128]{2,1,0:T(8,128)(2,1)} %copy-done.2), calls=%async_computation.3 | async-start | bytes 2097152 | tf_op jit(solution)/shard_map/all_to_all | solution.py:464
  113.3 11.4 %all-to-all-start.4 = ((f32[8,16,128]{2,1,0:T(8,128)}), f32[8,16,128]{2,1,0:T(8,128)S(1)}, u32[]{:S(2)}, u32[]{:S(2)}) async-start(f32[8,16,128]{2,1,0:T(8,128)} %score.1), calls=%async_computation.4 | async-start | bytes 131072 | tf_op jit(solution)/shard_map/all_to_all | solution.py:460
  119.9 46.5 %copy-start.7 = (bf16[2,128,256]{2,1,0:T(8,128)(2,1)S(1)}, bf16[2,128,256]{2,1,0:T(8,128)(2,1)}, u32[]{:S(2)}) copy-start(bf16[2,128,256]{2,1,0:T(8,128)(2,1)} %constant.40.clone.spread_ref) | copy-start | bytes 393220
  175.1 13.5 %all-to-all-start.6 = ((f32[8,2,32,128]{3,2,1,0:T(8,128)}), f32[8,2,32,128]{3,2,1,0:T(8,128)S(1)}, u32[]{:S(2)}, u32[]{:S(2)}) async-start(f32[8,2,32,128]{3,2,1,0:T(8,128)} %totals.1), calls=%async_computation.6 | async-start | bytes 524288 | tf_op jit(solution)/shard_map/all_to_all | solution.py:460
where the time goes:
time: 190 us
  blocking collectives  60 us (32%)
  waiting for transfers between devices  47.1 us (25%)
  Pallas kernels  37.2 us (20%)
  starting transfers between devices  35.2 us (19%)
  local copies, waits for them, and re-layouts  7.72 us (4%)
    all_to_all x2, blocking collectives, over_vol(): return lax.all_to_all(x, 'vol', split_axis=0, concat_axis=0, tiled=True)  60 us
    all_to_all x4, starting transfers between devices, over_img(): return lax.all_to_all(x, 'img', split_axis=0, concat_axis=0, tiled=True)  30.6 us
    all_to_all x1, waiting for transfers between devices, over_vol(): return lax.all_to_all(x, 'vol', split_axis=0, concat_axis=0, tiled=True)  26.5 us
    all_to_all x4, waiting for transfers between devices, over_img(): return lax.all_to_all(x, 'img', split_axis=0, concat_axis=0, tiled=True)  20.6 us
    pallas_call x1, Pallas kernels, per_device(): call(gather_kernel, (struct((2, N, 128)), struct((NV, 64, 128), BF)), 'sl...  9.37 us
    pallas_call x1, Pallas kernels, per_device(): call(total_kernel, struct((NG, 2, FJ, 128)), 'totals', scratch_shapes=[pl...  8.73 us
    pallas_call x1, Pallas kernels, per_device(): call(score_kernel, struct((NG, 16, 128)), 'score', grid=(4,), in_specs=[i...  6.2 us
    pallas_call x1, Pallas kernels, per_device(): call(back_kernel, (struct((64, 128)), struct((NV, 72, 128), BF)), 'backpr...  5.79 us
  transfers between devices with their start and end apart: 5, of which 5 were waited for; matrix products, arithmetic and copies ran while one was open for 1% of the time, Pallas kernels for 6%

commit v1 on v0

--- a/solution.py
+++ b/solution.py
@@ -17,6 +17,7 @@
 ROWS = 128
 CAP = 16
 FJ = N // NG
+UNROLL = 2
 TR = 16
 F32 = jnp.float32
 BF = jnp.bfloat16
@@ -96,8 +97,8 @@
     return out.reshape(2, 128, 256)
 
 
-def fill_lists(at_ref, tiles_ref, params_ref, o_ref):
-    tiles = jnp.concatenate([tiles_ref[:, b, :] for b in range(NB)], axis=1)
+def fill_lists(at_ref, tiles_ref, blocks_ref, shifts_ref, prec_ref, o_ref):
+    tiles = jnp.concatenate([tiles_ref[pl.ds(b, NV, stride=NB), :] for b in range(NB)], axis=1)
     at = at_ref[0]
     width = NB * ROWS
     lane = lanes((NV, width))
@@ -119,7 +120,7 @@
     codes = table.T[:CAP]
 
     mine = jnp.concatenate(
-        [tiles_ref[pl.ds(at, 1), b, :] for b in range(NB)], axis=1
+        [tiles_ref[pl.ds(at * NB + b, 1), :] for b in range(NB)], axis=1
     )
     owner = jnp.right_shift(mine, 10)
     hot = sub == owner
@@ -137,7 +138,18 @@
     read = dot_nt(digits, found)
     inv = read[0:1] * 32.0 + read[1:2] + read[2:3] - 1.0
     pos = pos.astype(F32)
-    params = params_ref[...]
+    moved = (shifts_ref[...] + 8).astype(F32)
+    eye = (lanes((8, 8)) == lax.broadcasted_iota(jnp.int32, (8, 8), 0)).astype(F32)
+    blocks = dot_nt(eye, blocks_ref[...].astype(F32), HI)
+    params = jnp.concatenate(
+        [
+            blocks[:, 0:1] * 32.0 + moved,
+            blocks[:, 1:2] * 32.0 + moved,
+            dot_nt(eye, prec_ref[...], HI),
+            jnp.zeros((8, 127 - 2 * TR), F32),
+        ],
+        axis=1,
+    )
     for k in range(NG):
         o_ref[k, 64:80] = codes
         for q in range(8):
@@ -148,7 +160,26 @@
         o_ref[k, 96:104] = params
 
 
-def first_kernel(at_ref, d_ref, t_ref, tiles_ref, params_ref, o_ref):
+def first_kernel(
+    at_ref, d_hbm, t_hbm, tiles_hbm, blocks_hbm, shifts_hbm, prec_hbm, o_ref,
+    d_ref, t_ref, tiles_ref, blocks_ref, shifts_ref, prec_ref, sems,
+):
+    pairs = (
+        (tiles_hbm, tiles_ref),
+        (blocks_hbm, blocks_ref),
+        (shifts_hbm, shifts_ref),
+        (prec_hbm, prec_ref),
+        (t_hbm, t_ref),
+        (d_hbm, d_ref),
+    )
+    copies = [pltpu.make_async_copy(a, b, sems.at[k]) for k, (a, b) in enumerate(pairs)]
+    for copy in copies:
+        copy.start()
+    for copy in copies[:4]:
+        copy.wait()
+    fill_lists(at_ref, tiles_ref, blocks_ref, shifts_ref, prec_ref, o_ref)
+    for copy in copies[4:]:
+        copy.wait()
     table = t_ref[...]
     rows = [dot32(d_ref[n0], table) for n0 in range(4)]
     for c in range(2):
@@ -157,7 +188,6 @@
             moved = swap4([rows[n0][:, at : at + 128] for n0 in range(4)])
             for lo in range(4):
                 o_ref[hi * 4 + lo, c * 32 : c * 32 + 32] = moved[lo]
-    fill_lists(at_ref, tiles_ref, params_ref, o_ref)
 
 
 def second_kernel(x_ref, w_ref, o_ref):
@@ -174,7 +204,14 @@
     return jnp.concatenate(rows, axis=0).astype(jnp.int32)
 
 
-def gather_kernel(x_ref, w_ref, fold_ref, lists_ref, f_ref, o_ref, half):
+def slot_rows(lists_ref):
+    by_slot = jnp.concatenate(
+        [lists_ref[2 * gh + h, 64:80] for h in range(2) for gh in range(4)], axis=0
+    )
+    return by_slot.T[:NV].astype(jnp.int32)
+
+
+def gather_kernel(x_ref, w_ref, fold_ref, lists_ref, f_ref, o_hbm, half, o_ref, sems):
     parts = []
     for c in range(2):
         moved = swap4([x_ref[:, c * 4 + k, :] for k in range(4)])
@@ -212,28 +249,42 @@
         ).astype(BF)
         packed = dot16(kept, fold_ref[...]).reshape(4, 2, 64, 128)
         low = lanes((4, 64, 128)) < 64
-        o_ref[pl.ds(nb * 4, 4)] = jnp.where(low, packed[:, 0], packed[:, 1]).astype(BF)
+        at = pl.ds(nb * 4, 4)
+        o_ref[at] = jnp.where(low, packed[:, 0], packed[:, 1]).astype(BF)
+        pltpu.make_async_copy(o_ref.at[at], o_hbm.at[at], sems.at[nb]).start()
         return carry
 
-    lax.fori_loop(0, 16, step, 0)
-
-
-def image_kernel(x_ref, o_ref):
+    lax.fori_loop(0, 16, step, 0, unroll=UNROLL)
+    for nb in range(16):
+        at = pl.ds(nb * 4, 4)
+        pltpu.make_async_copy(o_ref.at[at], o_hbm.at[at], sems.at[nb]).wait()
+
+
+def image_kernel(at_ref, x_ref, o_ref):
+    at = at_ref[0]
+    chip, core = at // 2, at % 2
     for hi in range(2):
         parts = [
             x_ref[a // 2, a % 2, :, hi * 128 : hi * 128 + 128].astype(F32) for a in range(4)
         ]
         moved = swap4(parts)
         for lo in range(4):
-            o_ref[hi * 4 + lo, 0] = moved[lo].astype(BF)
-
-
-def score_kernel(x_ref, s_ref, lists_ref, t_ref, o_ref, cp1, cp2, ce):
-    gh = pl.program_id(0)
-    data = s_ref[...].reshape(NV * CAP, 128)
+            target = hi * 4 + lo
+            other = jnp.where(core == target % 2, 0, 1)
+            o_ref[other, jnp.bitwise_and(target // 2 - chip, 3), 0] = moved[lo].astype(BF)
+
+
+def score_kernel(at_ref, x0, x1, x2, x3, s_ref, lists_ref, t_ref, o_ref, cp1, cp2, ce):
+    chip, core = at_ref[0] // 2, at_ref[0] % 2
     half_of = lanes((512, 128)) // 64
-    for h in range(2):
+    for k in range(8):
+        x_ref = (x0, x1, x2, x3)[k // 2]
+        rel = k % 2
+        gh = jnp.bitwise_and(chip - k // 2, 3)
+        h = jnp.bitwise_xor(core, rel)
         g = gh * 2 + h
+        at = pl.ds(pl.multiple_of(gh * CAP, CAP), CAP)
+        data = s_ref[:, at, :].reshape(NV * CAP, 128)
         inv = lists_ref[g, 80:88].astype(jnp.int32)
         sub = lax.broadcasted_iota(jnp.int32, (512, 128), 0)
         hot = jnp.concatenate(
@@ -248,43 +299,39 @@
             s_b = turned[b * ROWS : (b + 1) * ROWS]
             energy = jnp.sum(s_a * s_a, axis=0, keepdims=True)
             for ih in range(4):
-                image = x_ref[h, ih].astype(F32)
+                image = x_ref[rel, ih].astype(F32)
                 one = jnp.sum(s_a * image, axis=0, keepdims=True)
                 two = jnp.sum(s_b * image, axis=0, keepdims=True)
                 for lo in range(2):
-                    at = pl.ds(g * 8 + lo * 4 + ih, 1)
+                    at = pl.ds(g * 8 + ih * 2 + lo, 1)
                     cp1[b, at, :] = one
                     cp2[b, at, :] = two
                     ce[b, at, :] = energy
 
-    @pl.when(gh == 3)
-    def _():
-        full = (
-            dot32(cp1[...].reshape(256, 128), t_ref[0, 0])
-            + dot32(cp2[...].reshape(256, 128), t_ref[0, 1])
-            + dot32(ce[...].reshape(256, 128), jnp.full((128, 256), -0.25, F32))
-        ).reshape(NB, 64, 256)
-        group = lanes((64, 128)) // 32
-        first = lax.broadcasted_iota(jnp.int32, (64, 128), 0) % 8 < 4
-        table = jnp.zeros((64, 128), F32)
-        for b in range(NB):
-            own = jnp.where(first, full[b, :, :128], full[b, :, 128:])
-            table = jnp.where(group == b, own, table)
-        idx = lists_ref[:, 96:104].reshape(64, 128).astype(jnp.int32)
-        score = jnp.take_along_axis(table, jnp.bitwise_and(idx, 127), axis=1)
-        group = lanes((16, 128)) // 32
-        packed = score[:16]
-        for q in range(1, 4):
-            packed = jnp.where(group == q, pltpu.roll(score[q * 16 : q * 16 + 16], 32 * q, 1), packed)
-        for k in range(NG):
-            o_ref[k] = packed
-
-
-def back_kernel(x_ref, p_ref, lists_ref, u_ref, w_ref, o_ref, fr, fi, rows):
-    gh = pl.program_id(0)
-
-    @pl.when(gh == 0)
-    def _():
+    full = (
+        dot32(cp1[...].reshape(256, 128), t_ref[0, 0])
+        + dot32(cp2[...].reshape(256, 128), t_ref[0, 1])
+        + dot32(ce[...].reshape(256, 128), jnp.full((128, 256), -0.25, F32))
+    ).reshape(NB, 64, 256)
+    group = lanes((64, 128)) // 32
+    first = lax.broadcasted_iota(jnp.int32, (64, 128), 0) % 2 == 0
+    table = jnp.zeros((64, 128), F32)
+    for b in range(NB):
+        own = jnp.where(first, full[b, :, :128], full[b, :, 128:])
+        table = jnp.where(group == b, own, table)
+    idx = lists_ref[:, 96:104].reshape(64, 128).astype(jnp.int32)
+    score = jnp.take_along_axis(table, jnp.bitwise_and(idx, 127), axis=1)
+    group = lanes((16, 128)) // 32
+    packed = score[:16]
+    for q in range(1, 4):
+        packed = jnp.where(group == q, pltpu.roll(score[q * 16 : q * 16 + 16], 32 * q, 1), packed)
+    for k in range(NG):
+        o_ref[k] = packed
+
+
+def back_kernel(at_ref, x0, x1, x2, x3, p_ref, lists_ref, u_ref, w_ref, o_ref, fr, fi, rows):
+    chip, core = at_ref[0] // 2, at_ref[0] % 2
+    if True:
         packed = p_ref[0]
         for k in range(1, NG):
             packed = packed + p_ref[k]
@@ -312,7 +359,7 @@
         for b in range(NB):
             for part, ref in ((0, fr), (1, fi)):
                 val = fac[b, :, part * 128 : part * 128 + 128]
-                val = jnp.where(low, val, pltpu.roll(val, 60, 0))
+                val = jnp.where(low, val, pltpu.roll(val, 63, 0))
                 ref[b] = val.astype(BF).astype(F32)
         block_of = (
             lanes((8, 128)) // 32 == lax.broadcasted_iota(jnp.int32, (8, 128), 0)
@@ -333,49 +380,39 @@
         )
         o_ref[:, 64:72] = jnp.broadcast_to(mass.reshape(1, 1, 128), (NV, 8, 128)).astype(BF)
 
-    low = lanes((NV * CAP, 128)) < 64
-    outs = []
-    for h in range(2):
-        g = gh * 2 + h
-        for b in range(NB):
-            acc_a = jnp.zeros((ROWS, 128), F32)
-            acc_b = jnp.zeros((ROWS, 128), F32)
-            for ih in range(4):
-                image = x_ref[h, ih].astype(F32)
-                at = pl.ds(g * 8 + ih, 1)
-                acc_a = acc_a + image * fr[b, at, :]
-                acc_b = acc_b + image * fi[b, at, :]
-            acc = acc_a + pltpu.roll(acc_a, 64, 1)
-            acc_b = acc_b + pltpu.roll(acc_b, 64, 1)
-            rows[b * ROWS : (b + 1) * ROWS] = (acc + pltpu.roll(acc_b, 32, 1)).astype(BF)
-        pos = lists_ref[g, 88:92].astype(jnp.int32)
-        sub = lax.broadcasted_iota(jnp.int32, (NV * CAP, 128), 0)
-        hot = jnp.concatenate(
-            [jnp.where(sub == pos[q : q + 1], 1.0, 0.0).astype(BF) for q in range(4)], axis=1
-        )
-        outs.append(dot16(hot, rows[...]))
-    at = pl.ds(pl.multiple_of(gh * CAP, CAP), CAP)
-    o_ref[:, at, :] = jnp.where(low, outs[0], outs[1]).astype(BF).reshape(NV, CAP, 128)
-
-
-def total_kernel(x_ref, f_ref, spread_ref, lists_ref, o_ref, tot, msum, codes, slot_mass):
+    half_of = lanes((NV * CAP, 128)) // 64
+    for d in range(4):
+        x_ref = (x0, x1, x2, x3)[d]
+        gh = jnp.bitwise_and(chip - d, 3)
+        outs = []
+        for rel in range(2):
+            g = gh * 2 + jnp.bitwise_xor(core, rel)
+            for b in range(NB):
+                acc_a = jnp.zeros((ROWS, 128), F32)
+                acc_b = jnp.zeros((ROWS, 128), F32)
+                for ih in range(4):
+                    image = x_ref[rel, ih].astype(F32)
+                    at = pl.ds(g * 8 + ih * 2, 1)
+                    acc_a = acc_a + image * fr[b, at, :]
+                    acc_b = acc_b + image * fi[b, at, :]
+                acc = acc_a + pltpu.roll(acc_a, 64, 1)
+                acc_b = acc_b + pltpu.roll(acc_b, 64, 1)
+                rows[rel, b * ROWS : (b + 1) * ROWS] = (acc + pltpu.roll(acc_b, 32, 1)).astype(BF)
+            pos = lists_ref[g, 88:92].astype(jnp.int32)
+            sub = lax.broadcasted_iota(jnp.int32, (NV * CAP, 128), 0)
+            hot = jnp.concatenate(
+                [jnp.where(sub == pos[q : q + 1], 1.0, 0.0).astype(BF) for q in range(4)], axis=1
+            )
+            outs.append(dot16(hot, rows[rel]))
+        at = pl.ds(pl.multiple_of(gh * CAP, CAP), CAP)
+        out = jnp.where(half_of == core, outs[0], outs[1])
+        o_ref[:, at, :] = out.astype(BF).reshape(NV, CAP, 128)
+
+
+def total_kernel(x_ref, f_ref, spread_ref, lists_ref, o_ref, tot, codes):
     tot[...] = jnp.zeros_like(tot)
-    msum[...] = jnp.zeros_like(msum)
     columns = slot_columns(lists_ref)
-    by_slot = jnp.concatenate(
-        [lists_ref[2 * gh + h, 64:80] for h in range(2) for gh in range(4)], axis=0
-    )
-    code = by_slot.T[:NV].astype(jnp.int32)
-    codes[...] = code
-    sent = x_ref[:, 64:72, :].astype(F32)[:, 0, :]
-    source = lax.broadcasted_iota(jnp.int32, (128, 128), 0)
-    target = lanes((128, 128))
-    group = target % 64 // 16 * 2 + target // 64
-    mass = jnp.zeros((NV, 128), F32)
-    for b in range(NB):
-        pick = (source % 32 == group * 4 + b).astype(F32)
-        mass = jnp.where(jnp.right_shift(code, 10) == b, dot32(sent, pick), mass)
-    slot_mass[...] = mass
+    codes[...] = slot_rows(lists_ref)
 
     def step(nb, carry):
         cols = pltpu.roll(columns, 128 - 4 * nb, 1)
@@ -401,53 +438,66 @@
         kept = jnp.concatenate(
             [kept[h][v * 64 : v * 64 + 64] for v in range(4) for h in range(2)], axis=0
         )
-        hots, weights = [], []
-        for v in range(4):
-            at = pl.ds(nb * 4 + v, 1)
-            row = codes[at, :]
-            mass = slot_mass[at, :]
-            hots.append(
+        sub = lax.broadcasted_iota(jnp.int32, (N, 128), 0)
+        hot = jnp.concatenate(
+            [
                 jnp.where(
-                    lax.broadcasted_iota(jnp.int32, (N, 128), 0) == jnp.bitwise_and(row, N - 1),
-                    1.0,
-                    0.0,
+                    sub == jnp.bitwise_and(codes[pl.ds(nb * 4 + v, 1), :], N - 1), 1.0, 0.0
                 ).astype(BF)
-            )
-            sub = lax.broadcasted_iota(jnp.int32, (8, 128), 0)
-            hit = (sub % 4 == jnp.bitwise_and(jnp.right_shift(row, 8), 3)) & (row >= 0)
-            upper = mass.astype(BF).astype(F32)
-            weights.append(
-                jnp.where(hit, jnp.where(sub < 4, upper, mass - upper), 0.0).astype(BF)
-            )
-        hot = jnp.concatenate(hots, axis=1)
+                for v in range(4)
+            ],
+            axis=1,
+        )
         tot[...] += dot16(hot, kept)
-        msum[...] += dot_nt(hot, jnp.concatenate(weights, axis=1))
         return carry
 
-    lax.fori_loop(0, 16, step, 0)
-    expand = (
-        lanes((8, 128)) // 32 == lax.broadcasted_iota(jnp.int32, (8, 128), 0) % 4
-    ).astype(F32)
-    scale = 1.0 / (1.0 + dot32(msum[...], expand))
+    lax.fori_loop(0, 16, step, 0, unroll=UNROLL)
     for c in range(2):
-        new = (tot[:, c * 128 : c * 128 + 128] + f_ref[c]) * scale
+        new = (tot[:, c * 128 : c * 128 + 128] + f_ref[c]).astype(BF)
         o_ref[:, c] = new.reshape(NG, FJ, 128)
 
 
-def last_kernel(x_ref, o_ref):
+def mass_kernel(at_ref, sent_ref, lists_ref, o_ref):
+    code = slot_rows(lists_ref)
+    sent = sent_ref[:, 0, :].astype(F32)
+    source = lax.broadcasted_iota(jnp.int32, (128, 128), 0)
+    target = lanes((128, 128))
+    group = target % 64 // 16 * 2 + target // 64
+    mass = jnp.zeros((NV, 128), F32)
+    for b in range(NB):
+        pick = (source % 32 == group * 4 + b).astype(F32)
+        mass = jnp.where(jnp.right_shift(code, 10) == b, dot32(sent, pick), mass)
+    sub = lax.broadcasted_iota(jnp.int32, (FJ, 128), 0) + at_ref[0] * FJ
+    total = [jnp.zeros((FJ, 128), F32) for _ in range(SLAB)]
+    for v in range(NV):
+        row = code[v : v + 1]
+        k1 = jnp.where(row < 0, -1, jnp.bitwise_and(jnp.right_shift(row, 8), 3))
+        hot = sub == jnp.bitwise_and(row, N - 1)
+        for k in range(SLAB):
+            share = jnp.where(k1 == k, mass[v : v + 1], 0.0)
+            total[k] = total[k] + jnp.where(hot, share, 0.0)
+    lane = lanes((FJ, 128))
+    out = jnp.ones((FJ, 128), F32)
+    for k in range(SLAB):
+        out = jnp.where(lane == k, 1.0 + jnp.sum(total[k], axis=1, keepdims=True), out)
+    o_ref[...] = out
+
+
+def last_kernel(x_ref, m_ref, o_ref):
+    scale = 1.0 / m_ref[...]
     for c in range(2):
         for hi in range(2):
-            moved = swap4([x_ref[hi * 4 + lo, c] for lo in range(4)])
+            moved = swap4([x_ref[hi * 4 + lo, c].astype(F32) for lo in range(4)])
             for k in range(4):
-                o_ref[k, :, c, hi * 128 : hi * 128 + 128] = moved[k]
-
-
-def call(kernel, out, name, **extra):
+                o_ref[k, :, c, hi * 128 : hi * 128 + 128] = moved[k] * scale[:, k : k + 1]
+
+
+def call(kernel, out, name, vmem_bytes=VM, **extra):
     return pl.pallas_call(
         kernel,
         out_shape=out,
         name=name,
-        compiler_params=pltpu.CompilerParams(vmem_limit_bytes=VM),
+        compiler_params=pltpu.CompilerParams(vmem_limit_bytes=vmem_bytes),
         **extra,
     )
 
@@ -489,107 +539,108 @@
     back_t = lax.dynamic_slice_in_dim(jnp.asarray(back_t), img_at, 1, 0)
     smem = pl.BlockSpec(memory_space=pltpu.SMEM)
     vmem = pl.BlockSpec(memory_space=pltpu.VMEM)
-
-    idx = (image_blocks[:, :, None] * 32 + shifts[:, None, :] + 8).reshape(NG, 2 * TR)
-    params = jnp.concatenate(
-        [idx.astype(F32), precision[:, None], jnp.zeros((NG, 127 - 2 * TR), F32)], axis=1
-    )
-    params = params.reshape(4, 2, 128).transpose(1, 0, 2).reshape(8, 128)
+    hbm = pl.BlockSpec(memory_space=pltpu.HBM)
 
     one = call(
         first_kernel,
         struct((NG, 104, 128)),
         "third_index",
-        in_specs=[smem, vmem, vmem, vmem, vmem],
+        vmem_bytes=63 * 1000 * 1000,
+        in_specs=[smem] + [hbm] * 6,
+        scratch_shapes=[
+            pltpu.VMEM((4, FJ, N), F32),
+            pltpu.VMEM((N, 2 * N), F32),
+            pltpu.VMEM((NV * NB, ROWS), jnp.int32),
+            pltpu.VMEM((2, NG), jnp.int32),
+            pltpu.VMEM((NG, TR), jnp.int32),
+            pltpu.VMEM((1, NG), F32),
+            pltpu.SemaphoreType.DMA((6,)),
+        ],
     )(
         vol_at.reshape(1).astype(jnp.int32),
         density,
         table_first(),
-        block_tiles.reshape(NV, NB, ROWS),
-        params,
+        block_tiles,
+        image_blocks.T,
+        shifts,
+        precision.reshape(1, NG),
     )
     images, one = lax.optimization_barrier((images, one))
     lists = over_img(one)
 
+    own_at = img_at.reshape(1).astype(jnp.int32)
     shared = call(
         image_kernel,
-        struct((NG, 4, ROWS, 128), BF),
+        struct((2, 4, 4, ROWS, 128), BF),
         "image_split",
         grid=(4,),
-        in_specs=[pl.BlockSpec((2, 2, ROWS, N), lambda i: (i, 0, 0, 0))],
-        out_specs=pl.BlockSpec((NG, 1, ROWS, 128), lambda i: (0, i, 0, 0)),
-    )(images)
+        in_specs=[smem, pl.BlockSpec((2, 2, ROWS, N), lambda i: (i, 0, 0, 0))],
+        out_specs=pl.BlockSpec((2, 4, 1, ROWS, 128), lambda i: (0, 0, i, 0, 0)),
+    )(own_at, images)
     lists, shared = lax.optimization_barrier((lists, shared))
+    sibling = lax.ppermute(shared[1], "img", [(i, i ^ 1) for i in range(NG)])
+    pairs = jnp.stack([shared[0], sibling], axis=1)
     two = call(second_kernel, struct((NV, 8, 128)), "second_index")(lists, table_second())
     two = over_vol(two)
-    two, shared = lax.optimization_barrier((two, shared))
-    shared = over_img(shared)
+    two, pairs = lax.optimization_barrier((two, pairs))
 
     fourier, outgoing = call(
         gather_kernel,
         (struct((2, N, 128)), struct((NV, 64, 128), BF)),
         "slice_tiles",
-        scratch_shapes=[pltpu.VMEM((N, N), BF)],
+        in_specs=[vmem] * 4,
+        out_specs=(vmem, hbm),
+        scratch_shapes=[
+            pltpu.VMEM((N, N), BF),
+            pltpu.VMEM((NV, 64, 128), BF),
+            pltpu.SemaphoreType.DMA((16,)),
+        ],
     )(two, table_third(), jnp.asarray(table_fold(), BF), lists)
-    incoming = over_vol(outgoing).reshape(NV, 4, CAP, 128)
-
-    def whole_spec(shape):
-        return pl.BlockSpec(shape, lambda i: (0,) * len(shape))
-
-    image_spec = pl.BlockSpec((2, 4, ROWS, 128), lambda i: (i, 0, 0, 0))
-    slot_spec = pl.BlockSpec((NV, 1, CAP, 128), lambda i: (0, i, 0, 0))
+    outgoing, pairs = lax.optimization_barrier((outgoing, pairs))
+    incoming = over_vol(outgoing)
+    from_chip = [pairs[0]] + [
+        lax.ppermute(pairs[d], "img", [(i, (i + 2 * d) % NG) for i in range(NG)])
+        for d in range(1, 4)
+    ]
+
     partial = call(
         score_kernel,
         struct((NG, 16, 128)),
         "score",
-        grid=(4,),
-        in_specs=[
-            image_spec,
-            slot_spec,
-            whole_spec((NG, 104, 128)),
-            whole_spec((1, 2, 128, 256)),
-        ],
-        out_specs=whole_spec((NG, 16, 128)),
+        in_specs=[smem] + [vmem] * 7,
         scratch_shapes=[pltpu.VMEM((NB, 64, 128), F32)] * 3,
-    )(shared, incoming, lists, score_t)
+    )(own_at, *from_chip, incoming, lists, score_t)
     partial = over_img(partial)
 
     weights, back = call(
         back_kernel,
         (struct((64, 128)), struct((NV, 72, 128), BF)),
         "backproject",
-        grid=(4,),
-        in_specs=[
-            image_spec,
-            whole_spec((NG, 16, 128)),
-            whole_spec((NG, 104, 128)),
-            whole_spec((1, 128, 256)),
-        ],
-        out_specs=(whole_spec((64, 128)), whole_spec((NV, 72, 128))),
+        in_specs=[smem] + [vmem] * 7,
         scratch_shapes=[
             pltpu.VMEM((NB, 64, 128), F32),
             pltpu.VMEM((NB, 64, 128), F32),
-            pltpu.VMEM((512, 128), BF),
+            pltpu.VMEM((2, 512, 128), BF),
         ],
-    )(shared, partial, lists, back_t)
+    )(own_at, *from_chip, partial, lists, back_t)
     returned = over_vol(back)
 
     updated = call(
         total_kernel,
-        struct((NG, 2, FJ, 128)),
+        struct((NG, 2, FJ, 128), BF),
         "totals",
-        scratch_shapes=[
-            pltpu.VMEM((N, N), F32),
-            pltpu.VMEM((N, 8), F32),
-            pltpu.VMEM((NV, 128), jnp.int32),
-            pltpu.VMEM((NV, 128), F32),
-        ],
+        scratch_shapes=[pltpu.VMEM((N, N), F32), pltpu.VMEM((NV, 128), jnp.int32)],
     )(returned, fourier, jnp.asarray(table_spread(), BF), lists)
+    sent = lax.slice_in_dim(returned, 64, 72, axis=1)
+    sent, updated = lax.optimization_barrier((sent, updated))
     updated = over_img(updated)
-    updated = call(last_kernel, struct((SLAB, FJ, 2, N)), "frequency_join")(updated)
+    masses = call(
+        mass_kernel, struct((FJ, 128)), "masses", in_specs=[smem, vmem, vmem]
+    )(own_at, sent, lists)
+    updated = call(last_kernel, struct((SLAB, FJ, 2, N)), "frequency_join")(updated, masses)
 
     own = lax.dynamic_slice_in_dim(weights, img_at * 8, 8, 0)[:, : 2 * TR]
-    posterior = own.reshape(2, 4, 2, TR).transpose(1, 0, 2, 3).reshape(NG, 2, TR)
+    posterior = own.reshape(NG, 2, TR)
     return (updated, posterior)
 
 

time: 190 us -> 173 us (0.911)
  blocking collectives: 60 us -> 35.7 us
  starting transfers between devices: 35.2 us -> 53.7 us
  waiting for transfers between devices: 47.1 us -> 43 us
  Pallas kernels: 37.2 us -> 33.7 us
  local copies, waits for them, and re-layouts: 7.72 us -> 4.39 us
    all_to_all x2 -> x1, blocking collectives: 60 us -> 35.7 us  [over_vol(): return lax.all_to_all(x, 'vol', split_axis=0, concat_axis=0, tiled=True)]
    all_to_all x1 -> x2, starting transfers between devices: 4.65 us -> 16.8 us  [over_vol(): return lax.all_to_all(x, 'vol', split_axis=0, concat_axis=0, tiled=True)]
    ppermute x0 -> x4, starting transfers between devices: none -> 11.3 us  [the longest x3 8.4 us: per_device(): lax.ppermute(pairs[d], 'img', [(i, (i + 2 * d) % NG) for i in range(NG)])]
    ppermute x0 -> x4, waiting for transfers between devices: none -> 8.73 us  [the longest x3 8.73 us: per_device(): lax.ppermute(pairs[d], 'img', [(i, (i + 2 * d) % NG) for i in range(NG)])]
    all_to_all x1 -> x2, waiting for transfers between devices: 26.5 us -> 19.3 us  [over_vol(): return lax.all_to_all(x, 'vol', split_axis=0, concat_axis=0, tiled=True)]
    all_to_all x4 -> x3, waiting for transfers between devices: 20.6 us -> 14.9 us  [over_img(): return lax.all_to_all(x, 'img', split_axis=0, concat_axis=0, tiled=True)]
    all_to_all x4 -> x3, starting transfers between devices: 30.6 us -> 25.6 us  [over_img(): return lax.all_to_all(x, 'img', split_axis=0, concat_axis=0, tiled=True)]
    unnamed x18 -> x10, local copies, waits for them, and re-layouts: 3.93 us -> 0.03 us
  transfers between devices with their start and end apart: 5 -> 9, of which waited for: 5 -> 8; matrix products, arithmetic and copies ran while one was open for 1% -> 3% of each run, Pallas kernels for 6% -> 2%
where the time goes in v1:
time: 173 us; the launch traced here: 172 us
  starting transfers between devices  53.7 us (31%)
  waiting for transfers between devices  43 us (25%)
  blocking collectives  35.7 us (21%)
  Pallas kernels  33.7 us (19%)
  local copies, waits for them, and re-layouts  4.39 us (3%)
    all_to_all x1, blocking collectives, over_vol(): return lax.all_to_all(x, 'vol', split_axis=0, concat_axis=0, tiled=True)  35.7 us
    all_to_all x3, starting transfers between devices, over_img(): return lax.all_to_all(x, 'img', split_axis=0, concat_axis=0, tiled=True)  25.6 us
    all_to_all x2, waiting for transfers between devices, over_vol(): return lax.all_to_all(x, 'vol', split_axis=0, concat_axis=0, tiled=True)  19.3 us
    all_to_all x2, starting transfers between devices, over_vol(): return lax.all_to_all(x, 'vol', split_axis=0, concat_axis=0, tiled=True)  16.8 us
    all_to_all x3, waiting for transfers between devices, over_img(): return lax.all_to_all(x, 'img', split_axis=0, concat_axis=0, tiled=True)  14.9 us
    ppermute x3, waiting for transfers between devices, per_device(): lax.ppermute(pairs[d], 'img', [(i, (i + 2 * d) % NG) for i in range(NG)])  8.73 us
    ppermute x3, starting transfers between devices, per_device(): lax.ppermute(pairs[d], 'img', [(i, (i + 2 * d) % NG) for i in range(NG)])  8.4 us
    pallas_call x1, Pallas kernels, per_device(): call(gather_kernel, (struct((2, N, 128)), struct((NV, 64, 128), BF)), 'sl...  7.3 us
  transfers between devices with their start and end apart: 9, of which 8 were waited for; matrix products, arithmetic and copies ran while one was open for 3% of the time, Pallas kernels for 2%

profile of v1, /device:TPU:1, one launch (start us, length us, event | category | flops | bytes accessed | tf_op | source)
XLA Modules:
  0.0 172.3 jit_solution(1979445989621690291)
XLA Ops:
  0.6 4.1 %third_index.1 = f32[8,104,128]{2,1,0:T(8,128)} custom-call(s32[1]{0:T(128)} %bitcast.1.at_ref, f32[4,32,256]{2,1,0:T(8,128)} %d_hbm.1, f32[256,512]{1,0:T(8,128)} %constant.31.clone.t_hbm, s32[256,128]{1,0:T(8,128)} %tiles_hbm.1, s32[2,8]{1,0:T(2,128)} %bitcast.19, s32[8,16]{1,0:T(8,128)} %shifts_hbm.1, f32[1,8]{1,0:T(1,128)} %bitcast.20), custom_call_target="tpu_custom_call" | custom-call | tf_op jit(solution)/shard_map/third_index/pallas_call | solution.py:544
  4.7 10.3 %all-to-all-start = ((f32[8,104,128]{2,1,0:T(8,128)}), f32[8,104,128]{2,1,0:T(8,128)S(1)}, u32[]{:S(2)}, u32[]{:S(2)}) async-start(f32[8,104,128]{2,1,0:T(8,128)} %third_index.1), calls=%async_computation | async-start | bytes 851968 | tf_op jit(solution)/shard_map/all_to_all | solution.py:510
  15.0 1.2 image_split.1
  16.2 7.2 %all-to-all-done.x_ref.lists_ref = f32[8,104,128]{2,1,0:T(8,128)S(1)} async-done(((f32[8,104,128]{2,1,0:T(8,128)}), f32[8,104,128]{2,1,0:T(8,128)S(1)}, u32[]{:S(2)}, u32[]{:S(2)}) %all-to-all-start) | async-done | bytes 426016 | tf_op jit(solution)/shard_map/all_to_all | solution.py:510
  23.4 0.9 slice_bitcast_fusion.1
  24.3 2.9 %collective-permute-start = (bf16[4,4,128,128]{3,2,1,0:T(8,128)(2,1)}, bf16[4,4,128,128]{3,2,1,0:T(8,128)(2,1)}, u32[]{:S(2)}, u32[]{:S(2)}) collective-permute-start(bf16[4,4,128,128]{3,2,1,0:T(8,128)(2,1)} %get-tuple-element.35), channel_id=1, source_target_pairs={{0,64},{64,0},{128,192},{192,128},{256,320},{320,256},{384,448},{4... | collective-permute-start | bytes 1572872 | tf_op jit(solution)/shard_map/ppermute | solution.py:581
  27.2 1.7 %second_index.1 = f32[64,8,128]{2,1,0:T(8,128)} custom-call(f32[8,104,128]{2,1,0:T(8,128)S(1)} %all-to-all-done.x_ref.lists_ref, f32[2,512,256]{2,1,0:T(8,128)S(1)} %copy-done.1), custom_call_target="tpu_custom_call" | custom-call | tf_op jit(solution)/shard_map/second_index/pallas_call | solution.py:583
  29.0 11.8 %all-to-all-start.1 = ((f32[64,8,128]{2,1,0:T(8,128)}), f32[64,8,128]{2,1,0:T(8,128)S(1)}, u32[]{:S(2)}, u32[]{:S(2)}) async-start(f32[64,8,128]{2,1,0:T(8,128)} %second_index.1), calls=%async_computation.1 | async-start | bytes 524288 | tf_op jit(solution)/shard_map/all_to_all | solution.py:514
  40.8 1.1 pad_maximum_fusion
  42.0 12.5 %all-to-all-done.1.x_ref = f32[64,8,128]{2,1,0:T(8,128)S(1)} async-done(((f32[64,8,128]{2,1,0:T(8,128)}), f32[64,8,128]{2,1,0:T(8,128)S(1)}, u32[]{:S(2)}, u32[]{:S(2)}) %all-to-all-start.1) | async-done | bytes 262176 | tf_op jit(solution)/shard_map/all_to_all | solution.py:514
  54.5 7.3 %slice_tiles.1 = (f32[2,256,128]{2,1,0:T(8,128)S(1)}, bf16[64,64,128]{2,1,0:T(8,128)(2,1)}) custom-call(f32[64,8,128]{2,1,0:T(8,128)S(1)} %all-to-all-done.1.x_ref, f32[2,256,256]{2,1,0:T(8,128)S(1)} %copy-done.2, bf16[256,128]{1,0:T(8,128)(2,1)S(1)} %copy-done.4, f32[8,104,128]{2,1,0:T(8,128)S(1)} %all-to-all-done.x_ref.lists_ref), custom_call_target="tpu_custom_call" | custom-call | tf_op jit(solution)/shard_map/slice_tiles/pallas_call | solution.py:587
  61.8 5.0 %all-to-all-start.2 = ((bf16[64,64,128]{2,1,0:T(8,128)(2,1)}), bf16[64,64,128]{2,1,0:T(8,128)(2,1)S(1)}, u32[]{:S(2)}, u32[]{:S(2)}) async-start(bf16[64,64,128]{2,1,0:T(8,128)(2,1)} %get-tuple-element.24), calls=%async_computation.2 | async-start | bytes 2097152 | tf_op jit(solution)/shard_map/all_to_all | solution.py:514
  66.7 0.9 slice_bitcast_fusion.2
  67.6 2.2 %collective-permute-start.1 = (bf16[2,4,128,128]{3,2,1,0:T(8,128)(2,1)}, bf16[2,4,128,128]{3,2,1,0:T(8,128)(2,1)S(1)}, u32[]{:S(2)}, u32[]{:S(2)}) collective-permute-start(bf16[2,4,128,128]{3,2,1,0:T(8,128)(2,1)} %get-tuple-element.32), channel_id=1, source_target_pairs={{0,128},{64,192},{128,256},{192,320},{256,384},{320,448},{384,0},{... | collective-permute-start | bytes 786440 | tf_op jit(solution)/shard_map/ppermute | solution.py:602
  69.8 3.7 %collective-permute-start.2 = (bf16[2,4,128,128]{3,2,1,0:T(8,128)(2,1)}, bf16[2,4,128,128]{3,2,1,0:T(8,128)(2,1)S(1)}, u32[]{:S(2)}, u32[]{:S(2)}) collective-permute-start(bf16[2,4,128,128]{3,2,1,0:T(8,128)(2,1)} %get-tuple-element.31), channel_id=1, source_target_pairs={{0,256},{64,320},{128,384},{192,448},{256,0},{320,64},{384,128},{4... | collective-permute-start | bytes 786440 | tf_op jit(solution)/shard_map/ppermute | solution.py:602
  73.5 2.5 %collective-permute-start.3 = (bf16[2,4,128,128]{3,2,1,0:T(8,128)(2,1)S(1)}, bf16[2,4,128,128]{3,2,1,0:T(8,128)(2,1)S(1)}, u32[]{:S(2)}, u32[]{:S(2)}) collective-permute-start(bf16[2,4,128,128]{3,2,1,0:T(8,128)(2,1)S(1)} %get-tuple-element.30), channel_id=1, source_target_pairs={{0,384},{64,448},{128,0},{192,64},{256,128},{320,192},{384,256},{4... | collective-permute-start | bytes 786440 | tf_op jit(solution)/shard_map/ppermute | solution.py:602
  76.1 1.0 constant_dynamic-slice_fusion.2.t_ref
  77.5 4.4 %collective-permute-done.2.x2 = bf16[2,4,128,128]{3,2,1,0:T(8,128)(2,1)S(1)} collective-permute-done((bf16[2,4,128,128]{3,2,1,0:T(8,128)(2,1)}, bf16[2,4,128,128]{3,2,1,0:T(8,128)(2,1)S(1)}, u32[]{:S(2)}, u32[]{:S(2)}) %collective-permute-start.2) | collective-permute-done | bytes 262176 | tf_op jit(solution)/shard_map/ppermute | solution.py:602
  81.9 3.9 %collective-permute-done.3.x3 = bf16[2,4,128,128]{3,2,1,0:T(8,128)(2,1)S(1)} collective-permute-done((bf16[2,4,128,128]{3,2,1,0:T(8,128)(2,1)S(1)}, bf16[2,4,128,128]{3,2,1,0:T(8,128)(2,1)S(1)}, u32[]{:S(2)}, u32[]{:S(2)}) %collective-permute-start.3) | collective-permute-done | bytes 262176 | tf_op jit(solution)/shard_map/ppermute | solution.py:602
  85.8 6.8 %all-to-all-done.2.s_ref = bf16[64,64,128]{2,1,0:T(8,128)(2,1)S(1)} async-done(((bf16[64,64,128]{2,1,0:T(8,128)(2,1)}), bf16[64,64,128]{2,1,0:T(8,128)(2,1)S(1)}, u32[]{:S(2)}, u32[]{:S(2)}) %all-to-all-start.2) | async-done | bytes 1048608 | tf_op jit(solution)/shard_map/all_to_all | solution.py:514
  92.6 5.5 %score.1 = f32[8,16,128]{2,1,0:T(8,128)} custom-call(s32[1]{0:T(128)} %bitcast.at_ref, bf16[2,4,128,128]{3,2,1,0:T(8,128)(2,1)S(1)} %get-tuple-element.33.x0, bf16[2,4,128,128]{3,2,1,0:T(8,128)(2,1)S(1)} %collective-permute-done.1.x1, bf16[2,4,128,128]{3,2,1,0:T(8,128)(2,1)S(1)} %collective-permute-done.2.x2, ...), custom_call_target="tpu_custom_call" | custom-call | tf_op jit(solution)/shard_map/score/pallas_call | solution.py:606
  98.1 8.4 %all-to-all-start.3 = ((f32[8,16,128]{2,1,0:T(8,128)}), f32[8,16,128]{2,1,0:T(8,128)S(1)}, u32[]{:S(2)}, u32[]{:S(2)}) async-start(f32[8,16,128]{2,1,0:T(8,128)} %score.1), calls=%async_computation.3 | async-start | bytes 131072 | tf_op jit(solution)/shard_map/all_to_all | solution.py:510
  106.5 0.9 constant_dynamic-slice_fusion.1.u_ref
  107.4 3.9 %all-to-all-done.3.p_ref = f32[8,16,128]{2,1,0:T(8,128)S(1)} async-done(((f32[8,16,128]{2,1,0:T(8,128)}), f32[8,16,128]{2,1,0:T(8,128)S(1)}, u32[]{:S(2)}, u32[]{:S(2)}) %all-to-all-start.3) | async-done | bytes 65568 | tf_op jit(solution)/shard_map/all_to_all | solution.py:510
  111.4 5.3 %backproject.1 = (f32[64,128]{1,0:T(8,128)S(1)}, bf16[64,72,128]{2,1,0:T(8,128)(2,1)S(1)}) custom-call(s32[1]{0:T(128)} %bitcast.at_ref, bf16[2,4,128,128]{3,2,1,0:T(8,128)(2,1)S(1)} %get-tuple-element.33.x0, bf16[2,4,128,128]{3,2,1,0:T(8,128)(2,1)S(1)} %collective-permute-done.1.x1, bf16[2,4,128,128]{3,2,1,0:T(8,128)(2,1)S(1)} %collective-permute-done.2.x2, ...), custom_call_target="tpu_custom_call" | custom-call | tf_op jit(solution)/shard_map/backproject/pallas_call | solution.py:615
  116.7 35.7 %all_to_all.30.x_ref = bf16[64,72,128]{2,1,0:T(8,128)(2,1)S(1)} all-to-all(bf16[64,72,128]{2,1,0:T(8,128)(2,1)S(1)} %get-tuple-element.25), channel_id=1, replica_groups=mesh['img'=8,'vol'=64] {'vol'}, dimensions={0} | all-to-all | bytes 2359296 | tf_op jit(solution)/shard_map/all_to_all | solution.py:514
  152.3 6.8 %totals.1 = bf16[8,2,32,128]{3,2,1,0:T(8,128)(2,1)} custom-call(bf16[64,72,128]{2,1,0:T(8,128)(2,1)S(1)} %all_to_all.30.x_ref, f32[2,256,128]{2,1,0:T(8,128)S(1)} %get-tuple-element.26.f_ref, bf16[2,128,256]{2,1,0:T(8,128)(2,1)S(1)} %copy-done.3, f32[8,104,128]{2,1,0:T(8,128)S(1)} %all-to-all-done.x_ref.lists_ref), custom_call_target="tpu_custom_call" | custom-call | tf_op jit(solution)/shard_map/totals/pallas_call | solution.py:628
  159.1 6.9 %all-to-all-start.5 = ((bf16[8,2,32,128]{3,2,1,0:T(8,128)(2,1)}), bf16[8,2,32,128]{3,2,1,0:T(8,128)(2,1)S(1)}, u32[]{:S(2)}, u32[]{:S(2)}) async-start(bf16[8,2,32,128]{3,2,1,0:T(8,128)(2,1)} %totals.1), calls=%async_computation.5 | async-start | bytes 262144 | tf_op jit(solution)/shard_map/all_to_all | solution.py:510
  166.0 0.7 reshape.19
  166.7 0.8 masses.1.m_ref
  167.5 3.8 %all-to-all-done.5.x_ref = bf16[8,2,32,128]{3,2,1,0:T(8,128)(2,1)S(1)} async-done(((bf16[8,2,32,128]{3,2,1,0:T(8,128)(2,1)}), bf16[8,2,32,128]{3,2,1,0:T(8,128)(2,1)S(1)}, u32[]{:S(2)}, u32[]{:S(2)}) %all-to-all-start.5) | async-done | bytes 131104 | tf_op jit(solution)/shard_map/all_to_all | solution.py:510
  171.3 1.0 frequency_join.1
  (14 shorter events, 0.5 us)
Async XLA Ops:
  0.6 14.3 %copy-start = (bf16[8,2,128,256]{3,2,1,0:T(8,128)(2,1)S(1)}, bf16[8,2,128,256]{3,2,1,0:T(8,128)(2,1)}, u32[]{:S(2)}) copy-start(bf16[8,2,128,256]{3,2,1,0:T(8,128)(2,1)} %x_ref) | copy-start | bytes 3145732
  4.7 18.7 %all-to-all-start = ((f32[8,104,128]{2,1,0:T(8,128)}), f32[8,104,128]{2,1,0:T(8,128)S(1)}, u32[]{:S(2)}, u32[]{:S(2)}) async-start(f32[8,104,128]{2,1,0:T(8,128)} %third_index.1), calls=%async_computation | async-start | bytes 851968 | tf_op jit(solution)/shard_map/all_to_all | solution.py:510
  16.2 11.0 %copy-start.1 = (f32[2,512,256]{2,1,0:T(8,128)S(1)}, f32[2,512,256]{2,1,0:T(8,128)}, u32[]{:S(2)}) copy-start(f32[2,512,256]{2,1,0:T(8,128)} %constant.32.clone.w_ref) | copy-start | bytes 3145732
  24.3 30.2 %copy-start.2 = (f32[2,256,256]{2,1,0:T(8,128)S(1)}, f32[2,256,256]{2,1,0:T(8,128)}, u32[]{:S(2)}) copy-start(f32[2,256,256]{2,1,0:T(8,128)} %constant.34.clone.w_ref) | copy-start | bytes 1572868
  24.3 30.2 %copy-start.4 = (bf16[256,128]{1,0:T(8,128)(2,1)S(1)}, bf16[256,128]{1,0:T(8,128)(2,1)}, u32[]{:S(2)}) copy-start(bf16[256,128]{1,0:T(8,128)(2,1)} %constant.33.clone.fold_ref) | copy-start | bytes 196612
  24.3 16.5 %collective-permute-start = (bf16[4,4,128,128]{3,2,1,0:T(8,128)(2,1)}, bf16[4,4,128,128]{3,2,1,0:T(8,128)(2,1)}, u32[]{:S(2)}, u32[]{:S(2)}) collective-permute-start(bf16[4,4,128,128]{3,2,1,0:T(8,128)(2,1)} %get-tuple-element.35), channel_id=1, source_target_pairs={{0,64},{64,0},{128,192},{192,128},{256,320},{320,256},{384,448},{4... | collective-permute-start | bytes 1572872 | tf_op jit(solution)/shard_map/ppermute | solution.py:581
  29.0 25.5 %all-to-all-start.1 = ((f32[64,8,128]{2,1,0:T(8,128)}), f32[64,8,128]{2,1,0:T(8,128)S(1)}, u32[]{:S(2)}, u32[]{:S(2)}) async-start(f32[64,8,128]{2,1,0:T(8,128)} %second_index.1), calls=%async_computation.1 | async-start | bytes 524288 | tf_op jit(solution)/shard_map/all_to_all | solution.py:514
  61.8 30.8 %all-to-all-start.2 = ((bf16[64,64,128]{2,1,0:T(8,128)(2,1)}), bf16[64,64,128]{2,1,0:T(8,128)(2,1)S(1)}, u32[]{:S(2)}, u32[]{:S(2)}) async-start(bf16[64,64,128]{2,1,0:T(8,128)(2,1)} %get-tuple-element.24), calls=%async_computation.2 | async-start | bytes 2097152 | tf_op jit(solution)/shard_map/all_to_all | solution.py:514
  67.6 9.9 %collective-permute-start.1 = (bf16[2,4,128,128]{3,2,1,0:T(8,128)(2,1)}, bf16[2,4,128,128]{3,2,1,0:T(8,128)(2,1)S(1)}, u32[]{:S(2)}, u32[]{:S(2)}) collective-permute-start(bf16[2,4,128,128]{3,2,1,0:T(8,128)(2,1)} %get-tuple-element.32), channel_id=1, source_target_pairs={{0,128},{64,192},{128,256},{192,320},{256,384},{320,448},{384,0},{... | collective-permute-start | bytes 786440 | tf_op jit(solution)/shard_map/ppermute | solution.py:602
  69.8 12.1 %collective-permute-start.2 = (bf16[2,4,128,128]{3,2,1,0:T(8,128)(2,1)}, bf16[2,4,128,128]{3,2,1,0:T(8,128)(2,1)S(1)}, u32[]{:S(2)}, u32[]{:S(2)}) collective-permute-start(bf16[2,4,128,128]{3,2,1,0:T(8,128)(2,1)} %get-tuple-element.31), channel_id=1, source_target_pairs={{0,256},{64,320},{128,384},{192,448},{256,0},{320,64},{384,128},{4... | collective-permute-start | bytes 786440 | tf_op jit(solution)/shard_map/ppermute | solution.py:602
  73.5 12.2 %collective-permute-start.3 = (bf16[2,4,128,128]{3,2,1,0:T(8,128)(2,1)S(1)}, bf16[2,4,128,128]{3,2,1,0:T(8,128)(2,1)S(1)}, u32[]{:S(2)}, u32[]{:S(2)}) collective-permute-start(bf16[2,4,128,128]{3,2,1,0:T(8,128)(2,1)S(1)} %get-tuple-element.30), channel_id=1, source_target_pairs={{0,384},{64,448},{128,0},{192,64},{256,128},{320,192},{384,256},{4... | collective-permute-start | bytes 786440 | tf_op jit(solution)/shard_map/ppermute | solution.py:602
  98.1 13.3 %all-to-all-start.3 = ((f32[8,16,128]{2,1,0:T(8,128)}), f32[8,16,128]{2,1,0:T(8,128)S(1)}, u32[]{:S(2)}, u32[]{:S(2)}) async-start(f32[8,16,128]{2,1,0:T(8,128)} %score.1), calls=%async_computation.3 | async-start | bytes 131072 | tf_op jit(solution)/shard_map/all_to_all | solution.py:510
  107.4 44.9 %copy-start.3 = (bf16[2,128,256]{2,1,0:T(8,128)(2,1)S(1)}, bf16[2,128,256]{2,1,0:T(8,128)(2,1)}, u32[]{:S(2)}) copy-start(bf16[2,128,256]{2,1,0:T(8,128)(2,1)} %constant.35.clone.spread_ref) | copy-start | bytes 393220
  159.1 12.2 %all-to-all-start.5 = ((bf16[8,2,32,128]{3,2,1,0:T(8,128)(2,1)}), bf16[8,2,32,128]{3,2,1,0:T(8,128)(2,1)S(1)}, u32[]{:S(2)}, u32[]{:S(2)}) async-start(bf16[8,2,32,128]{3,2,1,0:T(8,128)(2,1)} %totals.1), calls=%async_computation.5 | async-start | bytes 262144 | tf_op jit(solution)/shard_map/all_to_all | solution.py:510

commit v2 on v1

--- a/solution.py
+++ b/solution.py
@@ -17,12 +17,13 @@
 ROWS = 128
 CAP = 16
 FJ = N // NG
-UNROLL = 2
+POOL = 48
+UNROLL = 4
 TR = 16
 F32 = jnp.float32
 BF = jnp.bfloat16
 HI = lax.Precision.HIGHEST
-VM = 100 * 1024 * 1024 // 2
+VM = 24 * 1024 * 1024
 
 
 def dot32(a, b):
@@ -37,6 +38,10 @@
     return lax.dot_general(
         a, b, (((1,), (1,)), ((), ())), precision=precision, preferred_element_type=F32
     )
+
+
+def one_hot(a, b):
+    return jnp.where(a.astype(jnp.int16) == b.astype(jnp.int16), BF(1), BF(0))
 
 
 def lanes(shape):
@@ -95,6 +100,14 @@
             for j in range(32):
                 out[h, h, c, j, c, :, j] = 1.0
     return out.reshape(2, 128, 256)
+
+
+def quad_rows(table):
+    group = lanes((16, 128)) // 32
+    packed = table[:16]
+    for q in range(1, 4):
+        packed = jnp.where(group == q, pltpu.roll(table[q * 16 : q * 16 + 16], 32 * q, 1), packed)
+    return packed
 
 
 def fill_lists(at_ref, tiles_ref, blocks_ref, shifts_ref, prec_ref, o_ref):
@@ -138,6 +151,16 @@
     read = dot_nt(digits, found)
     inv = read[0:1] * 32.0 + read[1:2] + read[2:3] - 1.0
     pos = pos.astype(F32)
+    wide = lax.broadcasted_iota(jnp.int32, (128, width), 0) == owner
+    own_count = dot_nt(jnp.ones((8, width), BF), jnp.where(wide, 1.0, 0.0).astype(BF))
+    owners = jnp.right_shift(tiles, 10)
+    counts = jnp.zeros((NV, 128), F32)
+    for k in range(NV):
+        hits = jnp.where(owners == k, 1.0 if k < 32 else 256.0, 0.0)
+        hits = hits[:, :128] + hits[:, 128:256] + hits[:, 256:384] + hits[:, 384:]
+        hits = jnp.sum(hits, axis=1, keepdims=True)
+        counts = jnp.where(short == k % 32, counts + hits, counts)
+    pair_count = quad_rows(counts)
     moved = (shifts_ref[...] + 8).astype(F32)
     eye = (lanes((8, 8)) == lax.broadcasted_iota(jnp.int32, (8, 8), 0)).astype(F32)
     blocks = dot_nt(eye, blocks_ref[...].astype(F32), HI)
@@ -156,8 +179,9 @@
             o_ref[k, 80 + q : 81 + q] = inv[:, q * 128 : q * 128 + 128]
         for q in range(4):
             o_ref[k, 88 + q : 89 + q] = pos[:, q * 128 : q * 128 + 128]
-        o_ref[k, 92:96] = jnp.zeros((4, 128), F32)
+        o_ref[k, 92:96] = own_count[0:4]
         o_ref[k, 96:104] = params
+        o_ref[k, 104:120] = pair_count
 
 
 def first_kernel(
@@ -196,22 +220,46 @@
     o_ref[...] = (dot32(w_ref[0], re) + dot32(w_ref[1], im)).reshape(NV, 8, 128)
 
 
-def slot_columns(lists_ref):
-    low = lanes((CAP, 128)) < 64
-    rows = [
-        jnp.where(low, lists_ref[2 * gh, 64:80], lists_ref[2 * gh + 1, 64:80]) for gh in range(4)
-    ]
-    return jnp.concatenate(rows, axis=0).astype(jnp.int32)
-
-
-def slot_rows(lists_ref):
-    by_slot = jnp.concatenate(
-        [lists_ref[2 * gh + h, 64:80] for h in range(2) for gh in range(4)], axis=0
-    )
-    return by_slot.T[:NV].astype(jnp.int32)
-
-
-def gather_kernel(x_ref, w_ref, fold_ref, lists_ref, f_ref, o_hbm, half, o_ref, sems):
+def pool_kernel(lists_ref, cols_ref, offs_ref, flag_ref):
+    before = (
+        lanes((NG, NG)) < lax.broadcasted_iota(jnp.int32, (NG, NG), 0)
+    ).astype(F32)
+    counts = jnp.concatenate([lists_ref[g, 92:93] for g in range(NG)], axis=0)
+    offs_ref[0] = jnp.minimum(dot32(before, counts).astype(jnp.int32), 2 * POOL)
+    offs_ref[1] = lax.broadcasted_iota(jnp.int32, (NG, 128), 0) * CAP
+    pairs = lists_ref[0, 104:120]
+    for g in range(1, NG):
+        pairs = pairs + lists_ref[g, 104:120]
+    pairs = pairs.astype(jnp.int32)
+    most = jnp.maximum(jnp.bitwise_and(pairs, 255), jnp.right_shift(pairs, 8))
+    most = jnp.max(jnp.max(most, axis=0, keepdims=True), axis=1, keepdims=True)
+    flag_ref[...] = jnp.broadcast_to(jnp.where(most <= 2 * POOL - 1, 1, 0), (8, 128))
+    half = lanes((64, 128)) // 64
+    row = lax.broadcasted_iota(jnp.int32, (64, 128), 0)
+    place_a = jnp.where(row < POOL, row + half * POOL, -1)
+    place_b = row + half * 64
+    col_a = jnp.zeros((64, 128), jnp.int32)
+    col_b = jnp.zeros((64, 128), jnp.int32)
+    start = jnp.zeros((1, 128), jnp.int32)
+    for g in range(NG):
+        code = lists_ref[g, 64:80].astype(jnp.int32)
+        filled = jnp.where(code >= 0, code + 1 + 4096 * g, 0)
+        for s in range(CAP):
+            col_a = col_a + jnp.where(place_a == start + s, filled[s : s + 1], 0)
+            col_b = jnp.where(place_b == g * CAP + s, filled[s : s + 1], col_b)
+        start = start + jnp.sum(jnp.where(code >= 0, 1, 0), axis=0, keepdims=True)
+    cols_ref[0] = col_a - 1
+    cols_ref[1] = col_b - 1
+
+
+def slot_rows(columns):
+    wide = jnp.concatenate([columns, columns], axis=0).astype(F32).T
+    low = lanes((NV, 128)) < 64
+    return jnp.where(low, wide[:NV], wide[NV:]).astype(jnp.int32)
+
+
+def gather_kernel(x_ref, w_ref, fold_ref, cols_ref, f_ref, o_hbm, half, o_ref, sems):
+    rows = o_ref.shape[1]
     parts = []
     for c in range(2):
         moved = swap4([x_ref[:, c * 4 + k, :] for k in range(4)])
@@ -224,13 +272,13 @@
     half[:, :128] = f_re.astype(BF)
     half[:, 128:] = f_im.astype(BF)
 
-    columns = slot_columns(lists_ref)
+    columns = cols_ref[...]
 
     def step(nb, carry):
         cols = pltpu.roll(columns, 128 - 4 * nb, 1)
         tile = jnp.concatenate(
             [
-                jnp.broadcast_to(cols[:, 64 * h + v : 64 * h + v + 1], (64, 128))
+                jnp.broadcast_to(cols[:rows, 64 * h + v : 64 * h + v + 1], (rows, 128))
                 for v in range(4)
                 for h in range(2)
             ],
@@ -240,15 +288,15 @@
         k0 = jnp.bitwise_and(tile, N - 1)
         k1 = jnp.where(tile < 0, -1, jnp.bitwise_and(jnp.right_shift(tile, 8), 3))
         hot = jnp.concatenate(
-            [jnp.where(k0 == lane, 1.0, 0.0), jnp.where(k0 == lane + 128, 1.0, 0.0)], axis=1
-        ).astype(BF)
+            [one_hot(k0, lane), one_hot(k0, lane + 128)], axis=1
+        )
         got = dot16(hot, half[...])
         keep = k1 == lane // 32
         kept = jnp.concatenate(
             [jnp.where(keep, got[:, :128], 0.0), jnp.where(keep, got[:, 128:], 0.0)], axis=1
         ).astype(BF)
-        packed = dot16(kept, fold_ref[...]).reshape(4, 2, 64, 128)
-        low = lanes((4, 64, 128)) < 64
+        packed = dot16(kept, fold_ref[...]).reshape(4, 2, rows, 128)
+        low = lanes((4, rows, 128)) < 64
         at = pl.ds(nb * 4, 4)
         o_ref[at] = jnp.where(low, packed[:, 0], packed[:, 1]).astype(BF)
         pltpu.make_async_copy(o_ref.at[at], o_hbm.at[at], sems.at[nb]).start()
@@ -260,53 +308,65 @@
         pltpu.make_async_copy(o_ref.at[at], o_hbm.at[at], sems.at[nb]).wait()
 
 
-def image_kernel(at_ref, x_ref, o_ref):
-    at = at_ref[0]
-    chip, core = at // 2, at % 2
+def image_kernel(at_ref, x_ref, own_ref, other_ref):
+    chip, core = at_ref[0] // 2, at_ref[0] % 2
     for hi in range(2):
         parts = [
             x_ref[a // 2, a % 2, :, hi * 128 : hi * 128 + 128].astype(F32) for a in range(4)
         ]
-        moved = swap4(parts)
-        for lo in range(4):
-            target = hi * 4 + lo
-            other = jnp.where(core == target % 2, 0, 1)
-            o_ref[other, jnp.bitwise_and(target // 2 - chip, 3), 0] = moved[lo].astype(BF)
-
-
-def score_kernel(at_ref, x0, x1, x2, x3, s_ref, lists_ref, t_ref, o_ref, cp1, cp2, ce):
+        moved = [part.astype(BF) for part in swap4(parts)]
+        for lo in range(0, 4, 2):
+            offset = jnp.bitwise_and(hi * 2 + lo // 2 - chip, 3)
+            own_ref[offset, 0] = jnp.where(core == 0, moved[lo], moved[lo + 1])
+            other_ref[offset, 0] = jnp.where(core == 0, moved[lo + 1], moved[lo])
+
+
+def score_kernel(
+    at_ref, offs_ref, x0, x1, x2, x3, s_ref, lists_ref, t_ref, o_ref, cp1, cp2, ce, pool, slots
+):
     chip, core = at_ref[0] // 2, at_ref[0] % 2
-    half_of = lanes((512, 128)) // 64
+    rows_in = s_ref.shape[1]
+    low = lanes((8, rows_in, 128)) < 64
+
+    def spread(n, carry):
+        at = pl.ds(n * 8, 8)
+        got = s_ref[at].astype(F32)
+        back = pltpu.roll(got, 64, 2)
+        pool[at, 0:rows_in] = jnp.where(low, got, back)
+        pool[at, rows_in : 2 * rows_in] = jnp.where(low, back, got)
+        pool[at, 2 * rows_in :] = jnp.zeros((8, CAP, 128), F32)
+        return carry
+
+    lax.fori_loop(0, 8, spread, 0)
+
     for k in range(8):
         x_ref = (x0, x1, x2, x3)[k // 2]
         rel = k % 2
         gh = jnp.bitwise_and(chip - k // 2, 3)
         h = jnp.bitwise_xor(core, rel)
         g = gh * 2 + h
-        at = pl.ds(pl.multiple_of(gh * CAP, CAP), CAP)
-        data = s_ref[:, at, :].reshape(NV * CAP, 128)
+        for v in range(NV):
+            slots[v * CAP : (v + 1) * CAP] = pool[v, pl.ds(offs_ref[g, v], CAP), :].astype(BF)
+        data = slots[...]
         inv = lists_ref[g, 80:88].astype(jnp.int32)
         sub = lax.broadcasted_iota(jnp.int32, (512, 128), 0)
         hot = jnp.concatenate(
-            [jnp.where(sub == inv[q : q + 1], 1.0, 0.0).astype(BF) for q in range(8)], axis=1
+            [one_hot(sub, inv[q : q + 1]) for q in range(8)], axis=1
         )
-        got = dot16(hot, data)
-        got = jnp.where(half_of == h, got, 0.0)
-        rows = got + pltpu.roll(got, 64, 1)
+        rows = dot16(hot, data)
         turned = pltpu.roll(rows, 32, 1)
-        for b in range(NB):
-            s_a = rows[b * ROWS : (b + 1) * ROWS]
-            s_b = turned[b * ROWS : (b + 1) * ROWS]
-            energy = jnp.sum(s_a * s_a, axis=0, keepdims=True)
-            for ih in range(4):
-                image = x_ref[rel, ih].astype(F32)
-                one = jnp.sum(s_a * image, axis=0, keepdims=True)
-                two = jnp.sum(s_b * image, axis=0, keepdims=True)
+        parts = [slice(b * ROWS, (b + 1) * ROWS) for b in range(NB)]
+        energy = [jnp.sum(rows[p] * rows[p], axis=0, keepdims=True) for p in parts]
+        for ih in range(4):
+            image = x_ref[rel, ih].astype(F32)
+            for b in range(NB):
+                one = jnp.sum(rows[parts[b]] * image, axis=0, keepdims=True)
+                two = jnp.sum(turned[parts[b]] * image, axis=0, keepdims=True)
                 for lo in range(2):
                     at = pl.ds(g * 8 + ih * 2 + lo, 1)
                     cp1[b, at, :] = one
                     cp2[b, at, :] = two
-                    ce[b, at, :] = energy
+                    ce[b, at, :] = energy[b]
 
     full = (
         dot32(cp1[...].reshape(256, 128), t_ref[0, 0])
@@ -321,15 +381,14 @@
         table = jnp.where(group == b, own, table)
     idx = lists_ref[:, 96:104].reshape(64, 128).astype(jnp.int32)
     score = jnp.take_along_axis(table, jnp.bitwise_and(idx, 127), axis=1)
-    group = lanes((16, 128)) // 32
-    packed = score[:16]
-    for q in range(1, 4):
-        packed = jnp.where(group == q, pltpu.roll(score[q * 16 : q * 16 + 16], 32 * q, 1), packed)
+    packed = quad_rows(score)
     for k in range(NG):
         o_ref[k] = packed
 
 
-def back_kernel(at_ref, x0, x1, x2, x3, p_ref, lists_ref, u_ref, w_ref, o_ref, fr, fi, rows):
+def back_kernel(
+    at_ref, offs_ref, x0, x1, x2, x3, p_ref, lists_ref, u_ref, w_ref, o_ref, fr, fi, rows, pool
+):
     chip, core = at_ref[0] // 2, at_ref[0] % 2
     if True:
         packed = p_ref[0]
@@ -371,52 +430,67 @@
         lane = lanes((8, 128))
         mass = jnp.sum(jnp.where(sub == lane % 4, per_group, 0.0), axis=0, keepdims=True)
         upper = mass.astype(BF).astype(F32)
-        middle = (mass - upper).astype(BF).astype(F32)
-        piece = lanes((1, 128)) // 32
-        mass = jnp.where(
-            piece == 0,
-            upper,
-            jnp.where(piece == 1, middle, jnp.where(piece == 2, mass - upper - middle, 0.0)),
-        )
-        o_ref[:, 64:72] = jnp.broadcast_to(mass.reshape(1, 1, 128), (NV, 8, 128)).astype(BF)
-
-    half_of = lanes((NV * CAP, 128)) // 64
+        mass = jnp.where(lanes((1, 128)) // 32 == 2, upper, mass - upper)
+
+    pool[...] = jnp.zeros_like(pool)
     for d in range(4):
         x_ref = (x0, x1, x2, x3)[d]
         gh = jnp.bitwise_and(chip - d, 3)
-        outs = []
         for rel in range(2):
             g = gh * 2 + jnp.bitwise_xor(core, rel)
-            for b in range(NB):
-                acc_a = jnp.zeros((ROWS, 128), F32)
-                acc_b = jnp.zeros((ROWS, 128), F32)
-                for ih in range(4):
-                    image = x_ref[rel, ih].astype(F32)
-                    at = pl.ds(g * 8 + ih * 2, 1)
-                    acc_a = acc_a + image * fr[b, at, :]
-                    acc_b = acc_b + image * fi[b, at, :]
-                acc = acc_a + pltpu.roll(acc_a, 64, 1)
-                acc_b = acc_b + pltpu.roll(acc_b, 64, 1)
-                rows[rel, b * ROWS : (b + 1) * ROWS] = (acc + pltpu.roll(acc_b, 32, 1)).astype(BF)
+            for part in range(0, ROWS, 32):
+                images = [x_ref[rel, ih, part : part + 32].astype(F32) for ih in range(4)]
+                for b in range(NB):
+                    acc_a = jnp.zeros((32, 128), F32)
+                    acc_b = jnp.zeros((32, 128), F32)
+                    for ih in range(4):
+                        at = pl.ds(g * 8 + ih * 2, 1)
+                        acc_a = acc_a + images[ih] * fr[b, at, :]
+                        acc_b = acc_b + images[ih] * fi[b, at, :]
+                    acc = acc_a + pltpu.roll(acc_a, 64, 1)
+                    acc_b = acc_b + pltpu.roll(acc_b, 64, 1)
+                    first = b * ROWS + part
+                    rows[rel, first : first + 32] = (acc + pltpu.roll(acc_b, 32, 1)).astype(BF)
             pos = lists_ref[g, 88:92].astype(jnp.int32)
             sub = lax.broadcasted_iota(jnp.int32, (NV * CAP, 128), 0)
             hot = jnp.concatenate(
-                [jnp.where(sub == pos[q : q + 1], 1.0, 0.0).astype(BF) for q in range(4)], axis=1
+                [one_hot(sub, pos[q : q + 1]) for q in range(4)], axis=1
             )
-            outs.append(dot16(hot, rows[rel]))
-        at = pl.ds(pl.multiple_of(gh * CAP, CAP), CAP)
-        out = jnp.where(half_of == core, outs[0], outs[1])
-        o_ref[:, at, :] = out.astype(BF).reshape(NV, CAP, 128)
-
-
-def total_kernel(x_ref, f_ref, spread_ref, lists_ref, o_ref, tot, codes):
+            out = dot16(hot, rows[rel])
+            for v in range(NV):
+                at = pl.ds(offs_ref[g, v], CAP)
+                pool[v, at, :] = pool[v, at, :] + out[v * CAP : (v + 1) * CAP]
+    half_rows = (pool.shape[1] - CAP) // 2
+    low = lanes((8, half_rows, 128)) < 64
+    last = lax.broadcasted_iota(jnp.int32, (8, half_rows, 128), 1) == half_rows - 1
+    tight = half_rows == POOL
+
+    def fold(n, carry):
+        at = pl.ds(n * 8, 8)
+        out = jnp.where(low, pool[at, 0:half_rows], pool[at, half_rows : 2 * half_rows])
+        if tight:
+            out = jnp.where(last & jnp.logical_not(low), mass.reshape(1, 1, 128), out)
+        o_ref[at, 0:half_rows] = out.astype(BF)
+        return carry
+
+    lax.fori_loop(0, 8, fold, 0)
+    if not tight:
+        o_ref[:, half_rows:] = jnp.broadcast_to(mass.reshape(1, 1, 128), (NV, 8, 128)).astype(BF)
+
+
+def total_kernel(x_ref, f_ref, spread_ref, cols_ref, o_ref, tot, codes):
     tot[...] = jnp.zeros_like(tot)
-    columns = slot_columns(lists_ref)
-    codes[...] = slot_rows(lists_ref)
+    columns = cols_ref[...]
+    codes[...] = slot_rows(columns)
+    tight = x_ref.shape[1] == POOL
 
     def step(nb, carry):
         cols = pltpu.roll(columns, 128 - 4 * nb, 1)
-        data = x_ref[pl.ds(nb * 4, 4), 0:64, :].reshape(256, 128)
+        if tight:
+            fill = jnp.zeros((4, 64 - POOL, 128), BF)
+            data = jnp.concatenate([x_ref[pl.ds(nb * 4, 4)], fill], axis=1).reshape(256, 128)
+        else:
+            data = x_ref[pl.ds(nb * 4, 4), 0:64, :].reshape(256, 128)
         kept = []
         for h in range(2):
             col = jnp.concatenate(
@@ -441,9 +515,7 @@
         sub = lax.broadcasted_iota(jnp.int32, (N, 128), 0)
         hot = jnp.concatenate(
             [
-                jnp.where(
-                    sub == jnp.bitwise_and(codes[pl.ds(nb * 4 + v, 1), :], N - 1), 1.0, 0.0
-                ).astype(BF)
+                one_hot(sub, jnp.bitwise_and(codes[pl.ds(nb * 4 + v, 1), :], N - 1))
                 for v in range(4)
             ],
             axis=1,
@@ -457,16 +529,12 @@
         o_ref[:, c] = new.reshape(NG, FJ, 128)
 
 
-def mass_kernel(at_ref, sent_ref, lists_ref, o_ref):
-    code = slot_rows(lists_ref)
+def mass_kernel(at_ref, sent_ref, cols_ref, o_ref):
+    code = slot_rows(cols_ref[...])
     sent = sent_ref[:, 0, :].astype(F32)
-    source = lax.broadcasted_iota(jnp.int32, (128, 128), 0)
-    target = lanes((128, 128))
-    group = target % 64 // 16 * 2 + target // 64
-    mass = jnp.zeros((NV, 128), F32)
-    for b in range(NB):
-        pick = (source % 32 == group * 4 + b).astype(F32)
-        mass = jnp.where(jnp.right_shift(code, 10) == b, dot32(sent, pick), mass)
+    block = jnp.right_shift(code, 10)
+    sent = sent + pltpu.roll(sent, 96, 1)
+    mass = jnp.take_along_axis(sent, jnp.where(code >= 0, 64 + block, 0), axis=1)
     sub = lax.broadcasted_iota(jnp.int32, (FJ, 128), 0) + at_ref[0] * FJ
     total = [jnp.zeros((FJ, 128), F32) for _ in range(SLAB)]
     for v in range(NV):
@@ -531,7 +599,7 @@
     return score.reshape(NG, 2, 128, 256), back.reshape(NG, 128, 256)
 
 
-def per_device(density, images, block_tiles, image_blocks, shifts, precision):
+def pipeline(half_rows, density, images, block_tiles, image_blocks, shifts, precision):
     vol_at = lax.axis_index("vol")
     img_at = lax.axis_index("img")
     score_t, back_t = phase_tables()
@@ -543,7 +611,7 @@
 
     one = call(
         first_kernel,
-        struct((NG, 104, 128)),
+        struct((NG, 120, 128)),
         "third_index",
         vmem_bytes=63 * 1000 * 1000,
         in_specs=[smem] + [hbm] * 6,
@@ -569,60 +637,97 @@
     lists = over_img(one)
 
     own_at = img_at.reshape(1).astype(jnp.int32)
-    shared = call(
+    own, other = call(
         image_kernel,
-        struct((2, 4, 4, ROWS, 128), BF),
+        (struct((4, 4, ROWS, 128), BF),) * 2,
         "image_split",
         grid=(4,),
         in_specs=[smem, pl.BlockSpec((2, 2, ROWS, N), lambda i: (i, 0, 0, 0))],
-        out_specs=pl.BlockSpec((2, 4, 1, ROWS, 128), lambda i: (0, 0, i, 0, 0)),
+        out_specs=(pl.BlockSpec((4, 1, ROWS, 128), lambda i: (0, i, 0, 0)),) * 2,
     )(own_at, images)
-    lists, shared = lax.optimization_barrier((lists, shared))
-    sibling = lax.ppermute(shared[1], "img", [(i, i ^ 1) for i in range(NG)])
-    pairs = jnp.stack([shared[0], sibling], axis=1)
+    lists, own, other = lax.optimization_barrier((lists, own, other))
     two = call(second_kernel, struct((NV, 8, 128)), "second_index")(lists, table_second())
+    two, lists, other = lax.optimization_barrier((two, lists, other))
+    cols, offs, flag = call(
+        pool_kernel,
+        (
+            struct((2, 64, 128), jnp.int32),
+            struct((2, NG, 128), jnp.int32),
+            struct((8, 128), jnp.int32),
+        ),
+        "pools",
+    )(lists)
+    cols, other = lax.optimization_barrier((cols, other))
+    sibling = lax.ppermute(other, "img", [(i, i ^ 1) for i in range(NG)])
+    pairs = jnp.stack([own, sibling], axis=1)
     two = over_vol(two)
     two, pairs = lax.optimization_barrier((two, pairs))
 
+    return exchange(half_rows, own_at, two, pairs, lists, cols, offs, score_t, back_t), flag
+
+
+def per_device(*inputs):
+    img_at = lax.axis_index("img")
+    done, flag = pipeline(POOL, *inputs)
+    updated, weights = lax.cond(
+        flag[0, 0] > 0,
+        lambda done, *rest: done,
+        lambda done, *rest: pipeline(64, *rest)[0],
+        done,
+        *inputs,
+    )
+    own = lax.dynamic_slice_in_dim(weights, img_at * 8, 8, 0)[:, : 2 * TR]
+    posterior = own.reshape(NG, 2, TR)
+    return (updated, posterior)
+
+
+def exchange(rows, own_at, two, pairs, lists, cols, offs, score_t, back_t):
+    smem = pl.BlockSpec(memory_space=pltpu.SMEM)
+    vmem = pl.BlockSpec(memory_space=pltpu.VMEM)
+    hbm = pl.BlockSpec(memory_space=pltpu.HBM)
+    tight = rows == POOL
+    cols = cols[0 if tight else 1]
+    offs = offs[0 if tight else 1]
     fourier, outgoing = call(
         gather_kernel,
-        (struct((2, N, 128)), struct((NV, 64, 128), BF)),
+        (struct((2, N, 128)), struct((NV, rows, 128), BF)),
         "slice_tiles",
         in_specs=[vmem] * 4,
         out_specs=(vmem, hbm),
         scratch_shapes=[
             pltpu.VMEM((N, N), BF),
-            pltpu.VMEM((NV, 64, 128), BF),
+            pltpu.VMEM((NV, rows, 128), BF),
             pltpu.SemaphoreType.DMA((16,)),
         ],
-    )(two, table_third(), jnp.asarray(table_fold(), BF), lists)
+    )(two, table_third(), jnp.asarray(table_fold(), BF), cols)
     outgoing, pairs = lax.optimization_barrier((outgoing, pairs))
     incoming = over_vol(outgoing)
     from_chip = [pairs[0]] + [
         lax.ppermute(pairs[d], "img", [(i, (i + 2 * d) % NG) for i in range(NG)])
         for d in range(1, 4)
     ]
-
     partial = call(
         score_kernel,
         struct((NG, 16, 128)),
         "score",
-        in_specs=[smem] + [vmem] * 7,
-        scratch_shapes=[pltpu.VMEM((NB, 64, 128), F32)] * 3,
-    )(own_at, *from_chip, incoming, lists, score_t)
+        in_specs=[smem] * 2 + [vmem] * 7,
+        scratch_shapes=[pltpu.VMEM((NB, 64, 128), F32)] * 3
+        + [pltpu.VMEM((NV, 2 * rows + CAP, 128), F32), pltpu.VMEM((NV * CAP, 128), BF)],
+    )(own_at, offs, *from_chip, incoming, lists, score_t)
     partial = over_img(partial)
 
     weights, back = call(
         back_kernel,
-        (struct((64, 128)), struct((NV, 72, 128), BF)),
+        (struct((64, 128)), struct((NV, rows if tight else rows + 8, 128), BF)),
         "backproject",
-        in_specs=[smem] + [vmem] * 7,
+        in_specs=[smem] * 2 + [vmem] * 7,
         scratch_shapes=[
             pltpu.VMEM((NB, 64, 128), F32),
             pltpu.VMEM((NB, 64, 128), F32),
             pltpu.VMEM((2, 512, 128), BF),
+            pltpu.VMEM((NV, 2 * rows + CAP, 128), F32),
         ],
-    )(own_at, *from_chip, partial, lists, back_t)
+    )(own_at, offs, *from_chip, partial, lists, back_t)
     returned = over_vol(back)
 
     updated = call(
@@ -630,18 +735,16 @@
         struct((NG, 2, FJ, 128), BF),
         "totals",
         scratch_shapes=[pltpu.VMEM((N, N), F32), pltpu.VMEM((NV, 128), jnp.int32)],
-    )(returned, fourier, jnp.asarray(table_spread(), BF), lists)
-    sent = lax.slice_in_dim(returned, 64, 72, axis=1)
+    )(returned, fourier, jnp.asarray(table_spread(), BF), cols)
+    at = rows - 1 if tight else rows
+    sent = jnp.broadcast_to(lax.slice_in_dim(returned, at, at + 1, axis=1), (NV, 8, 128))
     sent, updated = lax.optimization_barrier((sent, updated))
     updated = over_img(updated)
     masses = call(
         mass_kernel, struct((FJ, 128)), "masses", in_specs=[smem, vmem, vmem]
-    )(own_at, sent, lists)
+    )(own_at, sent, cols)
     updated = call(last_kernel, struct((SLAB, FJ, 2, N)), "frequency_join")(updated, masses)
-
-    own = lax.dynamic_slice_in_dim(weights, img_at * 8, 8, 0)[:, : 2 * TR]
-    posterior = own.reshape(NG, 2, TR)
-    return (updated, posterior)
+    return updated, weights
 
 
 def solution(mesh):

time: 173 us -> 162 us (0.936)
  blocking collectives: 35.7 us -> 29.1 us
  waiting for transfers between devices: 43 us -> 36.6 us
  Pallas kernels: 33.7 us -> 35.5 us
    all_to_all x1, blocking collectives: 35.7 us -> 29.1 us  [over_vol(): return lax.all_to_all(x, 'vol', split_axis=0, concat_axis=0, tiled=True)]
    all_to_all x2, waiting for transfers between devices: 19.3 us -> 14.6 us  [over_vol(): return lax.all_to_all(x, 'vol', split_axis=0, concat_axis=0, tiled=True)]
    pallas_call x9 -> x10, Pallas kernels: 33.7 us -> 35.5 us  [the longest x1 6.42 us: exchange(): call(gather_kernel, (struct((2, N, 128)), struct((NV, rows, 128), BF)), '...]
  transfers between devices with their start and end apart: 9 -> 9, of which waited for: 8 -> 8; matrix products, arithmetic and copies ran while one was open for 3% -> 2% of each run, Pallas kernels for 2% -> 2%
where the time goes in v2:
time: 162 us; the launch traced here: 161 us
  starting transfers between devices  53 us (33%)
  waiting for transfers between devices  36.6 us (23%)
  Pallas kernels  35.5 us (22%)
  blocking collectives  29.1 us (18%)
  local copies, waits for them, and re-layouts  4.08 us (3%)
    all_to_all x1, blocking collectives, over_vol(): return lax.all_to_all(x, 'vol', split_axis=0, concat_axis=0, tiled=True)  29.1 us
    all_to_all x3, starting transfers between devices, over_img(): return lax.all_to_all(x, 'img', split_axis=0, concat_axis=0, tiled=True)  24.8 us
    all_to_all x2, starting transfers between devices, over_vol(): return lax.all_to_all(x, 'vol', split_axis=0, concat_axis=0, tiled=True)  16.8 us
    all_to_all x2, waiting for transfers between devices, over_vol(): return lax.all_to_all(x, 'vol', split_axis=0, concat_axis=0, tiled=True)  14.6 us
    all_to_all x3, waiting for transfers between devices, over_img(): return lax.all_to_all(x, 'img', split_axis=0, concat_axis=0, tiled=True)  13.7 us
    ppermute x3, starting transfers between devices, exchange(): lax.ppermute(pairs[d], 'img', [(i, (i + 2 * d) % NG) for i in range(NG)])  8.6 us
    ppermute x3, waiting for transfers between devices, exchange(): lax.ppermute(pairs[d], 'img', [(i, (i + 2 * d) % NG) for i in range(NG)])  8.24 us
    pallas_call x1, Pallas kernels, exchange(): call(gather_kernel, (struct((2, N, 128)), struct((NV, rows, 128), BF)), '...  6.42 us
  transfers between devices with their start and end apart: 9, of which 8 were waited for; matrix products, arithmetic and copies ran while one was open for 2% of the time, Pallas kernels for 2%

profile of v2, /device:TPU:1, one launch (start us, length us, event | category | flops | bytes accessed | tf_op | source)
XLA Modules:
  0.0 161.2 jit_solution(13633289962736179109)
XLA Ops:
  0.6 4.7 %third_index.3 = f32[8,120,128]{2,1,0:T(8,128)} custom-call(s32[1]{0:T(128)} %bitcast.12.at_ref, f32[4,32,256]{2,1,0:T(8,128)} %d_hbm.1, f32[256,512]{1,0:T(8,128)} %constant.46.clone.t_hbm, s32[256,128]{1,0:T(8,128)} %tiles_hbm.1, s32[2,8]{1,0:T(2,128)} %bitcast.50, s32[8,16]{1,0:T(8,128)} %shifts_hbm.1, f32[1,8]{1,0:T(1,128)} %bitcast.52), custom_call_target="tpu_custom_call" | custom-call | tf_op jit(solution)/shard_map/third_index/pallas_call | solution.py:612
  5.4 10.3 %all-to-all-start.6 = ((f32[8,120,128]{2,1,0:T(8,128)}), f32[8,120,128]{2,1,0:T(8,128)S(1)}, u32[]{:S(2)}, u32[]{:S(2)}) async-start(f32[8,120,128]{2,1,0:T(8,128)} %third_index.3), calls=%async_computation.6 | async-start | bytes 983040 | tf_op jit(solution)/shard_map/all_to_all | solution.py:578
  15.6 2.9 %image_split.3 = (bf16[4,4,128,128]{3,2,1,0:T(8,128)(2,1)S(1)}, bf16[4,4,128,128]{3,2,1,0:T(8,128)(2,1)S(1)}) custom-call(s32[1]{0:T(128)} %bitcast.15.at_ref, bf16[8,2,128,256]{3,2,1,0:T(8,128)(2,1)} %x_ref), custom_call_target="tpu_custom_call" | custom-call | tf_op jit(solution)/shard_map/image_split/pallas_call | solution.py:640
  18.5 6.2 %all-to-all-done.6.x_ref.lists_ref = f32[8,120,128]{2,1,0:T(8,128)S(1)} async-done(((f32[8,120,128]{2,1,0:T(8,128)}), f32[8,120,128]{2,1,0:T(8,128)S(1)}, u32[]{:S(2)}, u32[]{:S(2)}) %all-to-all-start.6) | async-done | bytes 491552 | tf_op jit(solution)/shard_map/all_to_all | solution.py:578
  24.8 1.7 %second_index.3 = f32[64,8,128]{2,1,0:T(8,128)} custom-call(f32[8,120,128]{2,1,0:T(8,128)S(1)} %all-to-all-done.6.x_ref.lists_ref, f32[2,512,256]{2,1,0:T(8,128)S(1)} %copy-done), custom_call_target="tpu_custom_call" | custom-call | tf_op jit(solution)/shard_map/second_index/pallas_call | solution.py:649
  26.5 0.7 pools.3
  27.2 2.8 %collective-permute-start.4 = (bf16[4,4,128,128]{3,2,1,0:T(8,128)(2,1)S(1)}, bf16[4,4,128,128]{3,2,1,0:T(8,128)(2,1)S(1)}, u32[]{:S(2)}, u32[]{:S(2)}) collective-permute-start(bf16[4,4,128,128]{3,2,1,0:T(8,128)(2,1)S(1)} %get-tuple-element.109), channel_id=1, source_target_pairs={{0,64},{64,0},{128,192},{192,128},{256,320},{320,256},{384,448},{4... | collective-permute-start | bytes 1572872 | tf_op jit(solution)/shard_map/ppermute | solution.py:661
  30.0 11.8 %all-to-all-start.7 = ((f32[64,8,128]{2,1,0:T(8,128)}), f32[64,8,128]{2,1,0:T(8,128)S(1)}, u32[]{:S(2)}, u32[]{:S(2)}) async-start(f32[64,8,128]{2,1,0:T(8,128)} %second_index.3), calls=%async_computation.7 | async-start | bytes 524288 | tf_op jit(solution)/shard_map/all_to_all | solution.py:582
  41.9 0.8 copy-done.6
  42.7 1.1 pad_maximum_fusion.1
  43.8 11.7 %all-to-all-done.7.x_ref = f32[64,8,128]{2,1,0:T(8,128)S(1)} async-done(((f32[64,8,128]{2,1,0:T(8,128)}), f32[64,8,128]{2,1,0:T(8,128)S(1)}, u32[]{:S(2)}, u32[]{:S(2)}) %all-to-all-start.7) | async-done | bytes 262176 | tf_op jit(solution)/shard_map/all_to_all | solution.py:582
  55.5 6.4 %slice_tiles.3 = (f32[2,256,128]{2,1,0:T(8,128)S(1)}, bf16[64,48,128]{2,1,0:T(8,128)(2,1)}) custom-call(f32[64,8,128]{2,1,0:T(8,128)S(1)} %all-to-all-done.7.x_ref, f32[2,256,256]{2,1,0:T(8,128)} %constant.49.clone.w_ref, bf16[256,128]{1,0:T(8,128)(2,1)S(1)} %copy-done.10, s32[64,128]{1,0:T(8,128)S(1)} %slice_bitcast_fusion.10.cols_ref), custom_call_target="tpu_custom_call" | custom-call | tf_op jit(solution)/shard_map/slice_tiles/pallas_call | solution.py:691
  62.0 5.0 %all-to-all-start.8 = ((bf16[64,48,128]{2,1,0:T(8,128)(2,1)}), bf16[64,48,128]{2,1,0:T(8,128)(2,1)S(1)}, u32[]{:S(2)}, u32[]{:S(2)}) async-start(bf16[64,48,128]{2,1,0:T(8,128)(2,1)} %get-tuple-element.115), calls=%async_computation.8 | async-start | bytes 1572864 | tf_op jit(solution)/shard_map/all_to_all | solution.py:582
  67.0 2.2 %collective-permute-start.5 = (bf16[2,4,128,128]{3,2,1,0:T(8,128)(2,1)S(1)}, bf16[2,4,128,128]{3,2,1,0:T(8,128)(2,1)S(1)}, u32[]{:S(2)}, u32[]{:S(2)}) collective-permute-start(bf16[2,4,128,128]{3,2,1,0:T(8,128)(2,1)S(1)} %get-tuple-element.129), channel_id=1, source_target_pairs={{0,128},{64,192},{128,256},{192,320},{256,384},{320,448},{384,0},{... | collective-permute-start | bytes 786440 | tf_op jit(solution)/shard_map/ppermute | solution.py:706
  69.2 3.7 %collective-permute-start.6 = (bf16[2,4,128,128]{3,2,1,0:T(8,128)(2,1)S(1)}, bf16[2,4,128,128]{3,2,1,0:T(8,128)(2,1)S(1)}, u32[]{:S(2)}, u32[]{:S(2)}) collective-permute-start(bf16[2,4,128,128]{3,2,1,0:T(8,128)(2,1)S(1)} %get-tuple-element.128), channel_id=1, source_target_pairs={{0,256},{64,320},{128,384},{192,448},{256,0},{320,64},{384,128},{4... | collective-permute-start | bytes 786440 | tf_op jit(solution)/shard_map/ppermute | solution.py:706
  72.9 2.7 %collective-permute-start.7 = (bf16[2,4,128,128]{3,2,1,0:T(8,128)(2,1)S(1)}, bf16[2,4,128,128]{3,2,1,0:T(8,128)(2,1)S(1)}, u32[]{:S(2)}, u32[]{:S(2)}) collective-permute-start(bf16[2,4,128,128]{3,2,1,0:T(8,128)(2,1)S(1)} %get-tuple-element.127), channel_id=1, source_target_pairs={{0,384},{64,448},{128,0},{192,64},{256,128},{320,192},{384,256},{4... | collective-permute-start | bytes 786440 | tf_op jit(solution)/shard_map/ppermute | solution.py:706
  75.6 1.0 constant_dynamic-slice_fusion.4.t_ref
  76.7 4.4 %collective-permute-done.6.x2 = bf16[2,4,128,128]{3,2,1,0:T(8,128)(2,1)S(1)} collective-permute-done((bf16[2,4,128,128]{3,2,1,0:T(8,128)(2,1)S(1)}, bf16[2,4,128,128]{3,2,1,0:T(8,128)(2,1)S(1)}, u32[]{:S(2)}, u32[]{:S(2)}) %collective-permute-start.6) | collective-permute-done | bytes 262176 | tf_op jit(solution)/shard_map/ppermute | solution.py:706
  81.1 3.8 %collective-permute-done.7.x3 = bf16[2,4,128,128]{3,2,1,0:T(8,128)(2,1)S(1)} collective-permute-done((bf16[2,4,128,128]{3,2,1,0:T(8,128)(2,1)S(1)}, bf16[2,4,128,128]{3,2,1,0:T(8,128)(2,1)S(1)}, u32[]{:S(2)}, u32[]{:S(2)}) %collective-permute-start.7) | collective-permute-done | bytes 262176 | tf_op jit(solution)/shard_map/ppermute | solution.py:706
  84.9 2.9 %all-to-all-done.8.s_ref = bf16[64,48,128]{2,1,0:T(8,128)(2,1)S(1)} async-done(((bf16[64,48,128]{2,1,0:T(8,128)(2,1)}), bf16[64,48,128]{2,1,0:T(8,128)(2,1)S(1)}, u32[]{:S(2)}, u32[]{:S(2)}) %all-to-all-start.8) | async-done | bytes 786464 | tf_op jit(solution)/shard_map/all_to_all | solution.py:582
  87.8 6.3 %score.3 = f32[8,16,128]{2,1,0:T(8,128)} custom-call(s32[1]{0:T(128)} %bitcast.15.at_ref, s32[8,128]{1,0:T(8,128)S(1)} %slice_bitcast_fusion.11.offs_ref, bf16[2,4,128,128]{3,2,1,0:T(8,128)(2,1)S(1)} %get-tuple-element.130.x0, bf16[2,4,128,128]{3,2,1,0:T(8,128)(2,1)S(1)} %collective-permute-done.5.x1, ...), custom_call_target="tpu_custom_call" | custom-call | tf_op jit(solution)/shard_map/score/pallas_call | solution.py:709
  94.1 8.1 %all-to-all-start.9 = ((f32[8,16,128]{2,1,0:T(8,128)}), f32[8,16,128]{2,1,0:T(8,128)S(1)}, u32[]{:S(2)}, u32[]{:S(2)}) async-start(f32[8,16,128]{2,1,0:T(8,128)} %score.3), calls=%async_computation.9 | async-start | bytes 131072 | tf_op jit(solution)/shard_map/all_to_all | solution.py:578
  102.2 0.9 constant_dynamic-slice_fusion.3.u_ref
  103.1 4.0 %all-to-all-done.9.p_ref = f32[8,16,128]{2,1,0:T(8,128)S(1)} async-done(((f32[8,16,128]{2,1,0:T(8,128)}), f32[8,16,128]{2,1,0:T(8,128)S(1)}, u32[]{:S(2)}, u32[]{:S(2)}) %all-to-all-start.9) | async-done | bytes 65568 | tf_op jit(solution)/shard_map/all_to_all | solution.py:578
  107.0 6.2 %backproject.3 = (f32[64,128]{1,0:T(8,128)S(1)}, bf16[64,48,128]{2,1,0:T(8,128)(2,1)S(1)}) custom-call(s32[1]{0:T(128)} %bitcast.15.at_ref, s32[8,128]{1,0:T(8,128)S(1)} %slice_bitcast_fusion.11.offs_ref, bf16[2,4,128,128]{3,2,1,0:T(8,128)(2,1)S(1)} %get-tuple-element.130.x0, bf16[2,4,128,128]{3,2,1,0:T(8,128)(2,1)S(1)} %collective-permute-done.5.x1, ...), custom_call_target="tpu_custom_call" | custom-call | tf_op jit(solution)/shard_map/backproject/pallas_call | solution.py:719
  113.3 29.1 %all_to_all.55.x_ref = bf16[64,48,128]{2,1,0:T(8,128)(2,1)S(1)} all-to-all(bf16[64,48,128]{2,1,0:T(8,128)(2,1)S(1)} %get-tuple-element.116), channel_id=1, replica_groups=mesh['img'=8,'vol'=64] {'vol'}, dimensions={0} | all-to-all | bytes 1572864 | tf_op jit(solution)/shard_map/all_to_all | solution.py:582
  142.5 4.9 %totals.3 = bf16[8,2,32,128]{3,2,1,0:T(8,128)(2,1)} custom-call(bf16[64,48,128]{2,1,0:T(8,128)(2,1)S(1)} %all_to_all.55.x_ref, f32[2,256,128]{2,1,0:T(8,128)S(1)} %get-tuple-element.117.f_ref, bf16[2,128,256]{2,1,0:T(8,128)(2,1)S(1)} %copy-done.7, s32[64,128]{1,0:T(8,128)S(1)} %slice_bitcast_fusion.10.cols_ref), custom_call_target="tpu_custom_call" | custom-call | tf_op jit(solution)/shard_map/totals/pallas_call | solution.py:733
  147.4 6.4 %all-to-all-start.11 = ((bf16[8,2,32,128]{3,2,1,0:T(8,128)(2,1)}), bf16[8,2,32,128]{3,2,1,0:T(8,128)(2,1)S(1)}, u32[]{:S(2)}, u32[]{:S(2)}) async-start(bf16[8,2,32,128]{3,2,1,0:T(8,128)(2,1)} %totals.3), calls=%async_computation.11 | async-start | bytes 262144 | tf_op jit(solution)/shard_map/all_to_all | solution.py:578
  155.0 0.6 masses.3.m_ref
  155.7 3.5 %all-to-all-done.11.x_ref = bf16[8,2,32,128]{3,2,1,0:T(8,128)(2,1)S(1)} async-done(((bf16[8,2,32,128]{3,2,1,0:T(8,128)(2,1)}), bf16[8,2,32,128]{3,2,1,0:T(8,128)(2,1)S(1)}, u32[]{:S(2)}, u32[]{:S(2)}) %all-to-all-start.11) | async-done | bytes 131104 | tf_op jit(solution)/shard_map/all_to_all | solution.py:578
  159.2 1.0 frequency_join.3
  160.5 0.7 reshape.32
  (34 shorter events, 1.1 us)
Async XLA Ops:
  0.6 24.2 %copy-start = (f32[2,512,256]{2,1,0:T(8,128)S(1)}, f32[2,512,256]{2,1,0:T(8,128)}, u32[]{:S(2)}) copy-start(f32[2,512,256]{2,1,0:T(8,128)} %constant.47.clone.w_ref) | copy-start | bytes 3145732
  5.4 19.4 %all-to-all-start.6 = ((f32[8,120,128]{2,1,0:T(8,128)}), f32[8,120,128]{2,1,0:T(8,128)S(1)}, u32[]{:S(2)}, u32[]{:S(2)}) async-start(f32[8,120,128]{2,1,0:T(8,128)} %third_index.3), calls=%async_computation.6 | async-start | bytes 983040 | tf_op jit(solution)/shard_map/all_to_all | solution.py:578
  24.8 30.7 %copy-start.10 = (bf16[256,128]{1,0:T(8,128)(2,1)S(1)}, bf16[256,128]{1,0:T(8,128)(2,1)}, u32[]{:S(2)}) copy-start(bf16[256,128]{1,0:T(8,128)(2,1)} %constant.48.clone.fold_ref) | copy-start | bytes 196612
  27.2 14.6 %collective-permute-start.4 = (bf16[4,4,128,128]{3,2,1,0:T(8,128)(2,1)S(1)}, bf16[4,4,128,128]{3,2,1,0:T(8,128)(2,1)S(1)}, u32[]{:S(2)}, u32[]{:S(2)}) collective-permute-start(bf16[4,4,128,128]{3,2,1,0:T(8,128)(2,1)S(1)} %get-tuple-element.109), channel_id=1, source_target_pairs={{0,64},{64,0},{128,192},{192,128},{256,320},{320,256},{384,448},{4... | collective-permute-start | bytes 1572872 | tf_op jit(solution)/shard_map/ppermute | solution.py:661
  30.0 25.5 %all-to-all-start.7 = ((f32[64,8,128]{2,1,0:T(8,128)}), f32[64,8,128]{2,1,0:T(8,128)S(1)}, u32[]{:S(2)}, u32[]{:S(2)}) async-start(f32[64,8,128]{2,1,0:T(8,128)} %second_index.3), calls=%async_computation.7 | async-start | bytes 524288 | tf_op jit(solution)/shard_map/all_to_all | solution.py:582
  41.9 0.8 copy-start.6
  62.0 25.9 %all-to-all-start.8 = ((bf16[64,48,128]{2,1,0:T(8,128)(2,1)}), bf16[64,48,128]{2,1,0:T(8,128)(2,1)S(1)}, u32[]{:S(2)}, u32[]{:S(2)}) async-start(bf16[64,48,128]{2,1,0:T(8,128)(2,1)} %get-tuple-element.115), calls=%async_computation.8 | async-start | bytes 1572864 | tf_op jit(solution)/shard_map/all_to_all | solution.py:582
  67.0 9.7 %collective-permute-start.5 = (bf16[2,4,128,128]{3,2,1,0:T(8,128)(2,1)S(1)}, bf16[2,4,128,128]{3,2,1,0:T(8,128)(2,1)S(1)}, u32[]{:S(2)}, u32[]{:S(2)}) collective-permute-start(bf16[2,4,128,128]{3,2,1,0:T(8,128)(2,1)S(1)} %get-tuple-element.129), channel_id=1, source_target_pairs={{0,128},{64,192},{128,256},{192,320},{256,384},{320,448},{384,0},{... | collective-permute-start | bytes 786440 | tf_op jit(solution)/shard_map/ppermute | solution.py:706
  69.2 11.9 %collective-permute-start.6 = (bf16[2,4,128,128]{3,2,1,0:T(8,128)(2,1)S(1)}, bf16[2,4,128,128]{3,2,1,0:T(8,128)(2,1)S(1)}, u32[]{:S(2)}, u32[]{:S(2)}) collective-permute-start(bf16[2,4,128,128]{3,2,1,0:T(8,128)(2,1)S(1)} %get-tuple-element.128), channel_id=1, source_target_pairs={{0,256},{64,320},{128,384},{192,448},{256,0},{320,64},{384,128},{4... | collective-permute-start | bytes 786440 | tf_op jit(solution)/shard_map/ppermute | solution.py:706
  72.9 12.0 %collective-permute-start.7 = (bf16[2,4,128,128]{3,2,1,0:T(8,128)(2,1)S(1)}, bf16[2,4,128,128]{3,2,1,0:T(8,128)(2,1)S(1)}, u32[]{:S(2)}, u32[]{:S(2)}) collective-permute-start(bf16[2,4,128,128]{3,2,1,0:T(8,128)(2,1)S(1)} %get-tuple-element.127), channel_id=1, source_target_pairs={{0,384},{64,448},{128,0},{192,64},{256,128},{320,192},{384,256},{4... | collective-permute-start | bytes 786440 | tf_op jit(solution)/shard_map/ppermute | solution.py:706
  94.1 48.4 %copy-start.7 = (bf16[2,128,256]{2,1,0:T(8,128)(2,1)S(1)}, bf16[2,128,256]{2,1,0:T(8,128)(2,1)}, u32[]{:S(2)}) copy-start(bf16[2,128,256]{2,1,0:T(8,128)(2,1)} %constant.50.clone.spread_ref) | copy-start | bytes 393220
  94.1 12.9 %all-to-all-start.9 = ((f32[8,16,128]{2,1,0:T(8,128)}), f32[8,16,128]{2,1,0:T(8,128)S(1)}, u32[]{:S(2)}, u32[]{:S(2)}) async-start(f32[8,16,128]{2,1,0:T(8,128)} %score.3), calls=%async_computation.9 | async-start | bytes 131072 | tf_op jit(solution)/shard_map/all_to_all | solution.py:578
  113.2 46.9 %copy-start.1 = (f32[2,512,256]{2,1,0:T(8,128)S(1)}, f32[2,512,256]{2,1,0:T(8,128)}, u32[]{:S(2)}) copy-start(f32[2,512,256]{2,1,0:T(8,128)} %constant.47.clone.w_ref) | copy-start | bytes 3145732
  113.3 46.9 %copy-start.2 = (f32[256,512]{1,0:T(8,128)S(1)}, f32[256,512]{1,0:T(8,128)}, u32[]{:S(2)}) copy-start(f32[256,512]{1,0:T(8,128)} %constant.46.clone.t_hbm) | copy-start | bytes 1572868
  113.3 46.9 %copy-start.3 = (f32[2,256,256]{2,1,0:T(8,128)S(1)}, f32[2,256,256]{2,1,0:T(8,128)}, u32[]{:S(2)}) copy-start(f32[2,256,256]{2,1,0:T(8,128)} %constant.49.clone.w_ref) | copy-start | bytes 1572868
  113.3 46.9 %copy-start.4 = (f32[4,32,256]{2,1,0:T(8,128)S(1)}, f32[4,32,256]{2,1,0:T(8,128)}, u32[]{:S(2)}) copy-start(f32[4,32,256]{2,1,0:T(8,128)} %d_hbm.1) | copy-start | bytes 393220
  113.3 46.9 %copy-start.5 = (s32[256,128]{1,0:T(8,128)S(1)}, s32[256,128]{1,0:T(8,128)}, u32[]{:S(2)}) copy-start(s32[256,128]{1,0:T(8,128)} %tiles_hbm.1) | copy-start | bytes 393220
  113.3 46.9 %copy-start.12 = (s32[8,16]{1,0:T(8,128)S(1)}, s32[8,16]{1,0:T(8,128)}, u32[]{:S(2)}) copy-start(s32[8,16]{1,0:T(8,128)} %shifts_hbm.1) | copy-start | bytes 1540
  113.3 46.9 %copy-start.13 = (s32[8,2]{0,1:T(2,128)S(1)}, s32[8,2]{0,1:T(2,128)}, u32[]{:S(2)}) copy-start(s32[8,2]{0,1:T(2,128)} %param.25) | copy-start | bytes 196
  113.3 46.9 %copy-start.14 = (f32[8]{0:T(128)S(1)}, f32[8]{0:T(128)}, u32[]{:S(2)}) copy-start(f32[8]{0:T(128)} %param.27) | copy-start | bytes 100
  147.4 11.7 %all-to-all-start.11 = ((bf16[8,2,32,128]{3,2,1,0:T(8,128)(2,1)}), bf16[8,2,32,128]{3,2,1,0:T(8,128)(2,1)S(1)}, u32[]{:S(2)}, u32[]{:S(2)}) async-start(bf16[8,2,32,128]{3,2,1,0:T(8,128)(2,1)} %totals.3), calls=%async_computation.11 | async-start | bytes 262144 | tf_op jit(solution)/shard_map/all_to_all | solution.py:578

commit v3 on v2

--- a/solution.py
+++ b/solution.py
@@ -117,8 +117,11 @@
     lane = lanes((NV, width))
     sub = lax.broadcasted_iota(jnp.int32, (NV, width), 0)
     earlier = jnp.where(
-        lax.broadcasted_iota(jnp.int32, (width, width), 0) < lanes((width, width)), 1.0, 0.0
-    ).astype(BF)
+        lax.broadcasted_iota(jnp.int32, (width, width), 0).astype(jnp.int16)
+        < lanes((width, width)).astype(jnp.int16),
+        BF(1),
+        BF(0),
+    )
 
     owned = jnp.right_shift(tiles, 10) == at
     rank = dot16(jnp.where(owned, 1.0, 0.0).astype(BF), earlier).astype(jnp.int32)
@@ -145,9 +148,7 @@
     digits = jnp.where(
         kind == 0, jnp.right_shift(row, 5), jnp.where(kind == 1, jnp.bitwise_and(row, 31), 1)
     ).astype(F32).astype(BF)
-    found = jnp.where(
-        lax.broadcasted_iota(jnp.int32, (NV * CAP, width), 0) == pos, 1.0, 0.0
-    ).astype(BF)
+    found = one_hot(lax.broadcasted_iota(jnp.int32, (NV * CAP, width), 0), pos)
     read = dot_nt(digits, found)
     inv = read[0:1] * 32.0 + read[1:2] + read[2:3] - 1.0
     pos = pos.astype(F32)
@@ -155,11 +156,11 @@
     own_count = dot_nt(jnp.ones((8, width), BF), jnp.where(wide, 1.0, 0.0).astype(BF))
     owners = jnp.right_shift(tiles, 10)
     counts = jnp.zeros((NV, 128), F32)
-    for k in range(NV):
-        hits = jnp.where(owners == k, 1.0 if k < 32 else 256.0, 0.0)
+    for k in range(32):
+        hits = jnp.where(owners == k, 1.0, jnp.where(owners == k + 32, 256.0, 0.0))
         hits = hits[:, :128] + hits[:, 128:256] + hits[:, 256:384] + hits[:, 384:]
         hits = jnp.sum(hits, axis=1, keepdims=True)
-        counts = jnp.where(short == k % 32, counts + hits, counts)
+        counts = jnp.where(short == k, hits, counts)
     pair_count = quad_rows(counts)
     moved = (shifts_ref[...] + 8).astype(F32)
     eye = (lanes((8, 8)) == lax.broadcasted_iota(jnp.int32, (8, 8), 0)).astype(F32)
@@ -220,7 +221,8 @@
     o_ref[...] = (dot32(w_ref[0], re) + dot32(w_ref[1], im)).reshape(NV, 8, 128)
 
 
-def pool_kernel(lists_ref, cols_ref, offs_ref, flag_ref):
+def pool_kernel(lists_ref, table_ref, cols_ref, offs_ref, flag_ref, near_ref):
+    near_ref[...] = table_ref[...]
     before = (
         lanes((NG, NG)) < lax.broadcasted_iota(jnp.int32, (NG, NG), 0)
     ).astype(F32)
@@ -273,6 +275,7 @@
     half[:, 128:] = f_im.astype(BF)
 
     columns = cols_ref[...]
+    columns = jnp.where(columns < 0, -1, jnp.bitwise_and(columns, 1023))
 
     def step(nb, carry):
         cols = pltpu.roll(columns, 128 - 4 * nb, 1)
@@ -286,7 +289,7 @@
         )
         lane = lanes(tile.shape)
         k0 = jnp.bitwise_and(tile, N - 1)
-        k1 = jnp.where(tile < 0, -1, jnp.bitwise_and(jnp.right_shift(tile, 8), 3))
+        k1 = jnp.right_shift(tile, 8)
         hot = jnp.concatenate(
             [one_hot(k0, lane), one_hot(k0, lane + 128)], axis=1
         )
@@ -481,6 +484,7 @@
 def total_kernel(x_ref, f_ref, spread_ref, cols_ref, o_ref, tot, codes):
     tot[...] = jnp.zeros_like(tot)
     columns = cols_ref[...]
+    columns = jnp.where(columns < 0, -1, jnp.bitwise_and(columns, 1023))
     codes[...] = slot_rows(columns)
     tight = x_ref.shape[1] == POOL
 
@@ -500,7 +504,7 @@
                 ],
                 axis=0,
             )
-            k1 = jnp.where(col < 0, -1, jnp.bitwise_and(jnp.right_shift(col, 8), 3))
+            k1 = jnp.right_shift(col, 8)
             keep = k1 == lanes((256, 128)) // 32
             wide = dot16(data, spread_ref[h])
             kept.append(
@@ -647,41 +651,39 @@
     )(own_at, images)
     lists, own, other = lax.optimization_barrier((lists, own, other))
     two = call(second_kernel, struct((NV, 8, 128)), "second_index")(lists, table_second())
-    two, lists, other = lax.optimization_barrier((two, lists, other))
-    cols, offs, flag = call(
+    two, other = lax.optimization_barrier((two, other))
+    sibling = lax.ppermute(other, "img", [(i, i ^ 1) for i in range(NG)])
+    cols, offs, flag, third = call(
         pool_kernel,
         (
             struct((2, 64, 128), jnp.int32),
             struct((2, NG, 128), jnp.int32),
             struct((8, 128), jnp.int32),
+            struct((2, N, N)),
         ),
         "pools",
-    )(lists)
-    cols, other = lax.optimization_barrier((cols, other))
-    sibling = lax.ppermute(other, "img", [(i, i ^ 1) for i in range(NG)])
+    )(lists, table_third())
     pairs = jnp.stack([own, sibling], axis=1)
     two = over_vol(two)
     two, pairs = lax.optimization_barrier((two, pairs))
 
-    return exchange(half_rows, own_at, two, pairs, lists, cols, offs, score_t, back_t), flag
+    done = exchange(half_rows, own_at, two, pairs, lists, cols, offs, third, score_t, back_t)
+    return done, flag
 
 
 def per_device(*inputs):
-    img_at = lax.axis_index("img")
     done, flag = pipeline(POOL, *inputs)
-    updated, weights = lax.cond(
+    updated, posterior = lax.cond(
         flag[0, 0] > 0,
         lambda done, *rest: done,
         lambda done, *rest: pipeline(64, *rest)[0],
         done,
         *inputs,
     )
-    own = lax.dynamic_slice_in_dim(weights, img_at * 8, 8, 0)[:, : 2 * TR]
-    posterior = own.reshape(NG, 2, TR)
     return (updated, posterior)
 
 
-def exchange(rows, own_at, two, pairs, lists, cols, offs, score_t, back_t):
+def exchange(rows, own_at, two, pairs, lists, cols, offs, third, score_t, back_t):
     smem = pl.BlockSpec(memory_space=pltpu.SMEM)
     vmem = pl.BlockSpec(memory_space=pltpu.VMEM)
     hbm = pl.BlockSpec(memory_space=pltpu.HBM)
@@ -699,7 +701,7 @@
             pltpu.VMEM((NV, rows, 128), BF),
             pltpu.SemaphoreType.DMA((16,)),
         ],
-    )(two, table_third(), jnp.asarray(table_fold(), BF), cols)
+    )(two, third, jnp.asarray(table_fold(), BF), cols)
     outgoing, pairs = lax.optimization_barrier((outgoing, pairs))
     incoming = over_vol(outgoing)
     from_chip = [pairs[0]] + [
@@ -744,7 +746,8 @@
         mass_kernel, struct((FJ, 128)), "masses", in_specs=[smem, vmem, vmem]
     )(own_at, sent, cols)
     updated = call(last_kernel, struct((SLAB, FJ, 2, N)), "frequency_join")(updated, masses)
-    return updated, weights
+    weights = lax.dynamic_slice_in_dim(weights, own_at[0] * 8, 8, 0)[:, : 2 * TR]
+    return lax.optimization_barrier((updated, weights.reshape(NG, 2, TR)))
 
 
 def solution(mesh):

time: 162 us -> 160 us (0.988)
  waiting for transfers between devices: 36.6 us -> 34.5 us
    all_to_all x2, waiting for transfers between devices: 14.6 us -> 12.7 us  [over_vol(): return lax.all_to_all(x, 'vol', split_axis=0, concat_axis=0, tiled=True)]
  transfers between devices with their start and end apart: 9 -> 9, of which waited for: 8 -> 7; matrix products, arithmetic and copies ran while one was open for 2% -> 3% of each run, Pallas kernels for 2% -> 3%
where the time goes in v3:
time: 160 us; the launch traced here: 159 us
  starting transfers between devices  53.2 us (33%)
  Pallas kernels  35.3 us (22%)
  waiting for transfers between devices  34.5 us (22%)
  blocking collectives  29.1 us (18%)
  local copies, waits for them, and re-layouts  3.29 us (2%)
  other arithmetic  2.13 us (1%)
    all_to_all x1, blocking collectives, over_vol(): return lax.all_to_all(x, 'vol', split_axis=0, concat_axis=0, tiled=True)  29.1 us
    all_to_all x3, starting transfers between devices, over_img(): return lax.all_to_all(x, 'img', split_axis=0, concat_axis=0, tiled=True)  24.8 us
    all_to_all x2, starting transfers between devices, over_vol(): return lax.all_to_all(x, 'vol', split_axis=0, concat_axis=0, tiled=True)  16.9 us
    all_to_all x3, waiting for transfers between devices, over_img(): return lax.all_to_all(x, 'img', split_axis=0, concat_axis=0, tiled=True)  13.6 us
    all_to_all x2, waiting for transfers between devices, over_vol(): return lax.all_to_all(x, 'vol', split_axis=0, concat_axis=0, tiled=True)  12.7 us
    ppermute x3, starting transfers between devices, exchange(): lax.ppermute(pairs[d], 'img', [(i, (i + 2 * d) % NG) for i in range(NG)])  8.6 us
    ppermute x3, waiting for transfers between devices, exchange(): lax.ppermute(pairs[d], 'img', [(i, (i + 2 * d) % NG) for i in range(NG)])  8.23 us
    pallas_call x1, Pallas kernels, exchange(): call(score_kernel, struct((NG, 16, 128)), 'score', in_specs=[smem] * 2 +...  6.27 us
  transfers between devices with their start and end apart: 9, of which 7 were waited for; matrix products, arithmetic and copies ran while one was open for 3% of the time, Pallas kernels for 3%

profile of v3, /device:TPU:1, one launch (start us, length us, event | category | flops | bytes accessed | tf_op | source)
XLA Modules:
  0.0 159.4 jit_solution(16729082271079378424)
XLA Ops:
  0.6 4.4 %third_index.3 = f32[8,120,128]{2,1,0:T(8,128)} custom-call(s32[1]{0:T(128)} %bitcast.12.at_ref, f32[4,32,256]{2,1,0:T(8,128)} %d_hbm.1, f32[256,512]{1,0:T(8,128)} %constant.48.clone.t_hbm, s32[256,128]{1,0:T(8,128)} %tiles_hbm.1, s32[2,8]{1,0:T(2,128)} %bitcast.51, s32[8,16]{1,0:T(8,128)} %shifts_hbm.1, f32[1,8]{1,0:T(1,128)} %bitcast.53), custom_call_target="tpu_custom_call" | custom-call | tf_op jit(solution)/shard_map/third_index/pallas_call | solution.py:616
  5.1 10.3 %all-to-all-start.6 = ((f32[8,120,128]{2,1,0:T(8,128)}), f32[8,120,128]{2,1,0:T(8,128)S(1)}, u32[]{:S(2)}, u32[]{:S(2)}) async-start(f32[8,120,128]{2,1,0:T(8,128)} %third_index.3), calls=%async_computation.6 | async-start | bytes 983040 | tf_op jit(solution)/shard_map/all_to_all | solution.py:582
  15.4 2.9 %image_split.3 = (bf16[4,4,128,128]{3,2,1,0:T(8,128)(2,1)S(1)}, bf16[4,4,128,128]{3,2,1,0:T(8,128)(2,1)S(1)}) custom-call(s32[1]{0:T(128)} %bitcast.15.at_ref, bf16[8,2,128,256]{3,2,1,0:T(8,128)(2,1)} %x_ref), custom_call_target="tpu_custom_call" | custom-call | tf_op jit(solution)/shard_map/image_split/pallas_call | solution.py:644
  18.3 6.2 %all-to-all-done.6.lists_ref.x_ref = f32[8,120,128]{2,1,0:T(8,128)S(1)} async-done(((f32[8,120,128]{2,1,0:T(8,128)}), f32[8,120,128]{2,1,0:T(8,128)S(1)}, u32[]{:S(2)}, u32[]{:S(2)}) %all-to-all-start.6) | async-done | bytes 491552 | tf_op jit(solution)/shard_map/all_to_all | solution.py:582
  24.5 1.7 %second_index.3 = f32[64,8,128]{2,1,0:T(8,128)} custom-call(f32[8,120,128]{2,1,0:T(8,128)S(1)} %all-to-all-done.6.lists_ref.x_ref, f32[2,512,256]{2,1,0:T(8,128)S(1)} %copy-done), custom_call_target="tpu_custom_call" | custom-call | tf_op jit(solution)/shard_map/second_index/pallas_call | solution.py:653
  26.3 2.9 %collective-permute-start.4 = (bf16[4,4,128,128]{3,2,1,0:T(8,128)(2,1)S(1)}, bf16[4,4,128,128]{3,2,1,0:T(8,128)(2,1)}, u32[]{:S(2)}, u32[]{:S(2)}) collective-permute-start(bf16[4,4,128,128]{3,2,1,0:T(8,128)(2,1)S(1)} %get-tuple-element.100), channel_id=1, source_target_pairs={{0,64},{64,0},{128,192},{192,128},{256,320},{320,256},{384,448},{4... | collective-permute-start | bytes 1572872 | tf_op jit(solution)/shard_map/ppermute | solution.py:655
  29.2 11.8 %all-to-all-start.7 = ((f32[64,8,128]{2,1,0:T(8,128)}), f32[64,8,128]{2,1,0:T(8,128)S(1)}, u32[]{:S(2)}, u32[]{:S(2)}) async-start(f32[64,8,128]{2,1,0:T(8,128)} %second_index.3), calls=%async_computation.7 | async-start | bytes 524288 | tf_op jit(solution)/shard_map/all_to_all | solution.py:586
  41.0 1.8 %pools.3 = (s32[2,64,128]{2,1,0:T(8,128)S(1)}, s32[2,8,128]{2,1,0:T(8,128)S(1)}, s32[8,128]{1,0:T(8,128)S(1)}, f32[2,256,256]{2,1,0:T(8,128)S(1)}) custom-call(f32[8,120,128]{2,1,0:T(8,128)S(1)} %all-to-all-done.6.lists_ref.x_ref, f32[2,256,256]{2,1,0:T(8,128)} %constant.50.clone.table_ref), custom_call_target="tpu_custom_call" | custom-call | tf_op jit(solution)/shard_map/pools/pallas_call | solution.py:656
  42.8 2.1 %pad_maximum_fusion.1 = bf16[4,2,4,128,128]{4,3,2,1,0:T(8,128)(2,1)} fusion(bf16[4,1,4,128,128]{4,3,2,1,0:T(8,128)(2,1)} %bitcast.19, bf16[4,1,4,128,128]{4,3,2,1,0:T(8,128)(2,1)S(1)} %bitcast.46), kind=kLoop, calls=%fused_computation.11 | loop fusion | flops 524288 | bytes 2097152 | tf_op jit(solution)/shard_map/stack | solution.py:666
  44.9 9.7 %all-to-all-done.7.x_ref = f32[64,8,128]{2,1,0:T(8,128)S(1)} async-done(((f32[64,8,128]{2,1,0:T(8,128)}), f32[64,8,128]{2,1,0:T(8,128)S(1)}, u32[]{:S(2)}, u32[]{:S(2)}) %all-to-all-start.7) | async-done | bytes 262176 | tf_op jit(solution)/shard_map/all_to_all | solution.py:586
  54.7 5.4 %slice_tiles.3 = (f32[2,256,128]{2,1,0:T(8,128)S(1)}, bf16[64,48,128]{2,1,0:T(8,128)(2,1)}) custom-call(f32[64,8,128]{2,1,0:T(8,128)S(1)} %all-to-all-done.7.x_ref, f32[2,256,256]{2,1,0:T(8,128)S(1)} %get-tuple-element.102.w_ref, bf16[256,128]{1,0:T(8,128)(2,1)S(1)} %copy-done.9, s32[64,128]{1,0:T(8,128)S(1)} %slice_bitcast_fusion.10.cols_ref), custom_call_target="tpu_custom_call" | custom-call | tf_op jit(solution)/shard_map/slice_tiles/pallas_call | solution.py:693
  60.1 5.1 %all-to-all-start.8 = ((bf16[64,48,128]{2,1,0:T(8,128)(2,1)}), bf16[64,48,128]{2,1,0:T(8,128)(2,1)S(1)}, u32[]{:S(2)}, u32[]{:S(2)}) async-start(bf16[64,48,128]{2,1,0:T(8,128)(2,1)} %get-tuple-element.107), calls=%async_computation.8 | async-start | bytes 1572864 | tf_op jit(solution)/shard_map/all_to_all | solution.py:586
  65.3 2.2 %collective-permute-start.5 = (bf16[2,4,128,128]{3,2,1,0:T(8,128)(2,1)S(1)}, bf16[2,4,128,128]{3,2,1,0:T(8,128)(2,1)S(1)}, u32[]{:S(2)}, u32[]{:S(2)}) collective-permute-start(bf16[2,4,128,128]{3,2,1,0:T(8,128)(2,1)S(1)} %get-tuple-element.125), channel_id=1, source_target_pairs={{0,128},{64,192},{128,256},{192,320},{256,384},{320,448},{384,0},{... | collective-permute-start | bytes 786440 | tf_op jit(solution)/shard_map/ppermute | solution.py:708
  67.5 3.7 %collective-permute-start.6 = (bf16[2,4,128,128]{3,2,1,0:T(8,128)(2,1)S(1)}, bf16[2,4,128,128]{3,2,1,0:T(8,128)(2,1)S(1)}, u32[]{:S(2)}, u32[]{:S(2)}) collective-permute-start(bf16[2,4,128,128]{3,2,1,0:T(8,128)(2,1)S(1)} %get-tuple-element.124), channel_id=1, source_target_pairs={{0,256},{64,320},{128,384},{192,448},{256,0},{320,64},{384,128},{4... | collective-permute-start | bytes 786440 | tf_op jit(solution)/shard_map/ppermute | solution.py:708
  71.2 2.7 %collective-permute-start.7 = (bf16[2,4,128,128]{3,2,1,0:T(8,128)(2,1)S(1)}, bf16[2,4,128,128]{3,2,1,0:T(8,128)(2,1)S(1)}, u32[]{:S(2)}, u32[]{:S(2)}) collective-permute-start(bf16[2,4,128,128]{3,2,1,0:T(8,128)(2,1)S(1)} %get-tuple-element.123), channel_id=1, source_target_pairs={{0,384},{64,448},{128,0},{192,64},{256,128},{320,192},{384,256},{4... | collective-permute-start | bytes 786440 | tf_op jit(solution)/shard_map/ppermute | solution.py:708
  73.9 1.0 constant_dynamic-slice_fusion.5.t_ref
  75.0 4.4 %collective-permute-done.6.x2 = bf16[2,4,128,128]{3,2,1,0:T(8,128)(2,1)S(1)} collective-permute-done((bf16[2,4,128,128]{3,2,1,0:T(8,128)(2,1)S(1)}, bf16[2,4,128,128]{3,2,1,0:T(8,128)(2,1)S(1)}, u32[]{:S(2)}, u32[]{:S(2)}) %collective-permute-start.6) | collective-permute-done | bytes 262176 | tf_op jit(solution)/shard_map/ppermute | solution.py:708
  79.4 3.8 %collective-permute-done.7.x3 = bf16[2,4,128,128]{3,2,1,0:T(8,128)(2,1)S(1)} collective-permute-done((bf16[2,4,128,128]{3,2,1,0:T(8,128)(2,1)S(1)}, bf16[2,4,128,128]{3,2,1,0:T(8,128)(2,1)S(1)}, u32[]{:S(2)}, u32[]{:S(2)}) %collective-permute-start.7) | collective-permute-done | bytes 262176 | tf_op jit(solution)/shard_map/ppermute | solution.py:708
  83.1 2.9 %all-to-all-done.8.s_ref = bf16[64,48,128]{2,1,0:T(8,128)(2,1)S(1)} async-done(((bf16[64,48,128]{2,1,0:T(8,128)(2,1)}), bf16[64,48,128]{2,1,0:T(8,128)(2,1)S(1)}, u32[]{:S(2)}, u32[]{:S(2)}) %all-to-all-start.8) | async-done | bytes 786464 | tf_op jit(solution)/shard_map/all_to_all | solution.py:586
  86.1 6.3 %score.3 = f32[8,16,128]{2,1,0:T(8,128)} custom-call(s32[1]{0:T(128)} %bitcast.15.at_ref, s32[8,128]{1,0:T(8,128)S(1)} %slice_bitcast_fusion.11.offs_ref, bf16[2,4,128,128]{3,2,1,0:T(8,128)(2,1)S(1)} %get-tuple-element.126.x0, bf16[2,4,128,128]{3,2,1,0:T(8,128)(2,1)S(1)} %collective-permute-done.5.x1, ...), custom_call_target="tpu_custom_call" | custom-call | tf_op jit(solution)/shard_map/score/pallas_call | solution.py:711
  92.3 8.1 %all-to-all-start.9 = ((f32[8,16,128]{2,1,0:T(8,128)}), f32[8,16,128]{2,1,0:T(8,128)S(1)}, u32[]{:S(2)}, u32[]{:S(2)}) async-start(f32[8,16,128]{2,1,0:T(8,128)} %score.3), calls=%async_computation.9 | async-start | bytes 131072 | tf_op jit(solution)/shard_map/all_to_all | solution.py:582
  100.5 0.9 constant_dynamic-slice_fusion.4.u_ref
  101.4 4.0 %all-to-all-done.9.p_ref = f32[8,16,128]{2,1,0:T(8,128)S(1)} async-done(((f32[8,16,128]{2,1,0:T(8,128)}), f32[8,16,128]{2,1,0:T(8,128)S(1)}, u32[]{:S(2)}, u32[]{:S(2)}) %all-to-all-start.9) | async-done | bytes 65568 | tf_op jit(solution)/shard_map/all_to_all | solution.py:582
  105.3 6.2 %backproject.3 = (f32[64,128]{1,0:T(8,128)S(1)}, bf16[64,48,128]{2,1,0:T(8,128)(2,1)S(1)}) custom-call(s32[1]{0:T(128)} %bitcast.15.at_ref, s32[8,128]{1,0:T(8,128)S(1)} %slice_bitcast_fusion.11.offs_ref, bf16[2,4,128,128]{3,2,1,0:T(8,128)(2,1)S(1)} %get-tuple-element.126.x0, bf16[2,4,128,128]{3,2,1,0:T(8,128)(2,1)S(1)} %collective-permute-done.5.x1, ...), custom_call_target="tpu_custom_call" | custom-call | tf_op jit(solution)/shard_map/backproject/pallas_call | solution.py:721
  111.6 29.1 %all_to_all.55.x_ref = bf16[64,48,128]{2,1,0:T(8,128)(2,1)S(1)} all-to-all(bf16[64,48,128]{2,1,0:T(8,128)(2,1)S(1)} %get-tuple-element.108), channel_id=1, replica_groups=mesh['img'=8,'vol'=64] {'vol'}, dimensions={0} | all-to-all | bytes 1572864 | tf_op jit(solution)/shard_map/all_to_all | solution.py:586
  140.8 4.9 %totals.3 = bf16[8,2,32,128]{3,2,1,0:T(8,128)(2,1)} custom-call(bf16[64,48,128]{2,1,0:T(8,128)(2,1)S(1)} %all_to_all.55.x_ref, f32[2,256,128]{2,1,0:T(8,128)S(1)} %get-tuple-element.109.f_ref, bf16[2,128,256]{2,1,0:T(8,128)(2,1)S(1)} %copy-done.6, s32[64,128]{1,0:T(8,128)S(1)} %slice_bitcast_fusion.10.cols_ref), custom_call_target="tpu_custom_call" | custom-call | tf_op jit(solution)/shard_map/totals/pallas_call | solution.py:735
  145.7 6.4 %all-to-all-start.11 = ((bf16[8,2,32,128]{3,2,1,0:T(8,128)(2,1)}), bf16[8,2,32,128]{3,2,1,0:T(8,128)(2,1)S(1)}, u32[]{:S(2)}, u32[]{:S(2)}) async-start(bf16[8,2,32,128]{3,2,1,0:T(8,128)(2,1)} %totals.3), calls=%async_computation.11 | async-start | bytes 262144 | tf_op jit(solution)/shard_map/all_to_all | solution.py:582
  152.2 0.5 slice.51
  153.4 0.6 masses.3.m_ref
  154.1 3.4 %all-to-all-done.11.x_ref = bf16[8,2,32,128]{3,2,1,0:T(8,128)(2,1)S(1)} async-done(((bf16[8,2,32,128]{3,2,1,0:T(8,128)(2,1)}), bf16[8,2,32,128]{3,2,1,0:T(8,128)(2,1)S(1)}, u32[]{:S(2)}, u32[]{:S(2)}) %all-to-all-start.11) | async-done | bytes 131104 | tf_op jit(solution)/shard_map/all_to_all | solution.py:582
  157.5 1.0 frequency_join.3
  158.8 0.6 copy-done.11
  (34 shorter events, 0.6 us)
Async XLA Ops:
  0.6 23.9 %copy-start = (f32[2,512,256]{2,1,0:T(8,128)S(1)}, f32[2,512,256]{2,1,0:T(8,128)}, u32[]{:S(2)}) copy-start(f32[2,512,256]{2,1,0:T(8,128)} %constant.49.clone.w_ref) | copy-start | bytes 3145732
  5.1 19.4 %all-to-all-start.6 = ((f32[8,120,128]{2,1,0:T(8,128)}), f32[8,120,128]{2,1,0:T(8,128)S(1)}, u32[]{:S(2)}, u32[]{:S(2)}) async-start(f32[8,120,128]{2,1,0:T(8,128)} %third_index.3), calls=%async_computation.6 | async-start | bytes 983040 | tf_op jit(solution)/shard_map/all_to_all | solution.py:582
  26.3 28.4 %copy-start.9 = (bf16[256,128]{1,0:T(8,128)(2,1)S(1)}, bf16[256,128]{1,0:T(8,128)(2,1)}, u32[]{:S(2)}) copy-start(bf16[256,128]{1,0:T(8,128)(2,1)} %constant.51.clone.fold_ref) | copy-start | bytes 196612
  26.3 16.5 %collective-permute-start.4 = (bf16[4,4,128,128]{3,2,1,0:T(8,128)(2,1)S(1)}, bf16[4,4,128,128]{3,2,1,0:T(8,128)(2,1)}, u32[]{:S(2)}, u32[]{:S(2)}) collective-permute-start(bf16[4,4,128,128]{3,2,1,0:T(8,128)(2,1)S(1)} %get-tuple-element.100), channel_id=1, source_target_pairs={{0,64},{64,0},{128,192},{192,128},{256,320},{320,256},{384,448},{4... | collective-permute-start | bytes 1572872 | tf_op jit(solution)/shard_map/ppermute | solution.py:655
  29.2 25.5 %all-to-all-start.7 = ((f32[64,8,128]{2,1,0:T(8,128)}), f32[64,8,128]{2,1,0:T(8,128)S(1)}, u32[]{:S(2)}, u32[]{:S(2)}) async-start(f32[64,8,128]{2,1,0:T(8,128)} %second_index.3), calls=%async_computation.7 | async-start | bytes 524288 | tf_op jit(solution)/shard_map/all_to_all | solution.py:586
  60.1 5.1 %copy-start.2 = (bf16[4,2,4,128,128]{4,3,2,1,0:T(8,128)(2,1)S(1)}, bf16[4,2,4,128,128]{4,3,2,1,0:T(8,128)(2,1)}, u32[]{:S(2)}) copy-start(bf16[4,2,4,128,128]{4,3,2,1,0:T(8,128)(2,1)} %pad_maximum_fusion.1) | copy-start | bytes 3145732
  60.1 25.9 %all-to-all-start.8 = ((bf16[64,48,128]{2,1,0:T(8,128)(2,1)}), bf16[64,48,128]{2,1,0:T(8,128)(2,1)S(1)}, u32[]{:S(2)}, u32[]{:S(2)}) async-start(bf16[64,48,128]{2,1,0:T(8,128)(2,1)} %get-tuple-element.107), calls=%async_computation.8 | async-start | bytes 1572864 | tf_op jit(solution)/shard_map/all_to_all | solution.py:586
  65.3 9.7 %collective-permute-start.5 = (bf16[2,4,128,128]{3,2,1,0:T(8,128)(2,1)S(1)}, bf16[2,4,128,128]{3,2,1,0:T(8,128)(2,1)S(1)}, u32[]{:S(2)}, u32[]{:S(2)}) collective-permute-start(bf16[2,4,128,128]{3,2,1,0:T(8,128)(2,1)S(1)} %get-tuple-element.125), channel_id=1, source_target_pairs={{0,128},{64,192},{128,256},{192,320},{256,384},{320,448},{384,0},{... | collective-permute-start | bytes 786440 | tf_op jit(solution)/shard_map/ppermute | solution.py:708
  67.5 11.9 %collective-permute-start.6 = (bf16[2,4,128,128]{3,2,1,0:T(8,128)(2,1)S(1)}, bf16[2,4,128,128]{3,2,1,0:T(8,128)(2,1)S(1)}, u32[]{:S(2)}, u32[]{:S(2)}) collective-permute-start(bf16[2,4,128,128]{3,2,1,0:T(8,128)(2,1)S(1)} %get-tuple-element.124), channel_id=1, source_target_pairs={{0,256},{64,320},{128,384},{192,448},{256,0},{320,64},{384,128},{4... | collective-permute-start | bytes 786440 | tf_op jit(solution)/shard_map/ppermute | solution.py:708
  71.2 11.9 %collective-permute-start.7 = (bf16[2,4,128,128]{3,2,1,0:T(8,128)(2,1)S(1)}, bf16[2,4,128,128]{3,2,1,0:T(8,128)(2,1)S(1)}, u32[]{:S(2)}, u32[]{:S(2)}) collective-permute-start(bf16[2,4,128,128]{3,2,1,0:T(8,128)(2,1)S(1)} %get-tuple-element.123), channel_id=1, source_target_pairs={{0,384},{64,448},{128,0},{192,64},{256,128},{320,192},{384,256},{4... | collective-permute-start | bytes 786440 | tf_op jit(solution)/shard_map/ppermute | solution.py:708
  92.3 48.5 %copy-start.6 = (bf16[2,128,256]{2,1,0:T(8,128)(2,1)S(1)}, bf16[2,128,256]{2,1,0:T(8,128)(2,1)}, u32[]{:S(2)}) copy-start(bf16[2,128,256]{2,1,0:T(8,128)(2,1)} %constant.52.clone.spread_ref) | copy-start | bytes 393220
  92.3 13.0 %all-to-all-start.9 = ((f32[8,16,128]{2,1,0:T(8,128)}), f32[8,16,128]{2,1,0:T(8,128)S(1)}, u32[]{:S(2)}, u32[]{:S(2)}) async-start(f32[8,16,128]{2,1,0:T(8,128)} %score.3), calls=%async_computation.9 | async-start | bytes 131072 | tf_op jit(solution)/shard_map/all_to_all | solution.py:582
  111.5 46.9 %copy-start.1 = (f32[2,512,256]{2,1,0:T(8,128)S(1)}, f32[2,512,256]{2,1,0:T(8,128)}, u32[]{:S(2)}) copy-start(f32[2,512,256]{2,1,0:T(8,128)} %constant.49.clone.w_ref) | copy-start | bytes 3145732
  111.6 46.9 %copy-start.3 = (f32[256,512]{1,0:T(8,128)S(1)}, f32[256,512]{1,0:T(8,128)}, u32[]{:S(2)}) copy-start(f32[256,512]{1,0:T(8,128)} %constant.48.clone.t_hbm) | copy-start | bytes 1572868
  111.6 46.9 %copy-start.4 = (f32[4,32,256]{2,1,0:T(8,128)S(1)}, f32[4,32,256]{2,1,0:T(8,128)}, u32[]{:S(2)}) copy-start(f32[4,32,256]{2,1,0:T(8,128)} %d_hbm.1) | copy-start | bytes 393220
  111.6 46.9 %copy-start.5 = (s32[256,128]{1,0:T(8,128)S(1)}, s32[256,128]{1,0:T(8,128)}, u32[]{:S(2)}) copy-start(s32[256,128]{1,0:T(8,128)} %tiles_hbm.1) | copy-start | bytes 393220
  111.6 46.9 %copy-start.10 = (s32[8,16]{1,0:T(8,128)S(1)}, s32[8,16]{1,0:T(8,128)}, u32[]{:S(2)}) copy-start(s32[8,16]{1,0:T(8,128)} %shifts_hbm.1) | copy-start | bytes 1540
  111.6 46.9 %copy-start.12 = (s32[8,2]{0,1:T(2,128)S(1)}, s32[8,2]{0,1:T(2,128)}, u32[]{:S(2)}) copy-start(s32[8,2]{0,1:T(2,128)} %param.25) | copy-start | bytes 196
  111.6 46.9 %copy-start.13 = (f32[8]{0:T(128)S(1)}, f32[8]{0:T(128)}, u32[]{:S(2)}) copy-start(f32[8]{0:T(128)} %param.27) | copy-start | bytes 100
  145.7 11.7 %all-to-all-start.11 = ((bf16[8,2,32,128]{3,2,1,0:T(8,128)(2,1)}), bf16[8,2,32,128]{3,2,1,0:T(8,128)(2,1)S(1)}, u32[]{:S(2)}, u32[]{:S(2)}) async-start(bf16[8,2,32,128]{3,2,1,0:T(8,128)(2,1)} %totals.3), calls=%async_computation.11 | async-start | bytes 262144 | tf_op jit(solution)/shard_map/all_to_all | solution.py:582
  158.8 0.6 copy-start.11
